TPU v7x, 256 devices: a whole 4x4x8 slice. The times are simulated.
256 devices in a mesh: dp: 32 (over x, z), seq: 8 (over y, core).
Axes of the slice: x: 4, y: 4, z: 8, core: 2. Of those that a mesh axis runs over, the one named last changes fastest.
Arguments:
- hidden: bfloat16 [32, 32, 128, 1152], P('dp', 'seq'), may hold values from -8 to 8
- spatial_qkv: bfloat16 [32, 32, 128, 1728], P('dp', 'seq'), may hold values from -60 to 60
- out_spatial: bfloat16 [576, 1152], P('seq', 'dp'), may hold values from -0.25 to 0.25
- qkv_temporal: bfloat16 [1152, 1728], P('seq', 'dp'), may hold values from -1 to 1
- out_temporal: bfloat16 [576, 1152], P('seq', 'dp'), may hold values from -0.25 to 0.25
- modulation: float32 [32, 3, 1152], P('dp'), may hold values from -2 to 4
- cotangent: bfloat16 [32, 32, 128, 1152], P('dp', 'seq'), may hold values from -6 to 6
- frame_count: int32 [32], P('dp'), may hold values from 16 to 32, as said below
- patch_height: int32 [32], P('dp'), may hold values from 2 to 16, as said below
- patch_width: int32 [32], P('dp'), may hold values from 8 to 32, as said below
Outputs:
- block_out: bfloat16 [32, 32, 128, 1152], P('dp', 'seq')
- hidden_grad: bfloat16 [32, 32, 128, 1152], P('dp', 'seq')
- spatial_qkv_grad: bfloat16 [32, 32, 128, 1728], P('dp', 'seq')
- out_spatial_grad: float32 [576, 1152], P('seq', 'dp')
- qkv_temporal_grad: float32 [1152, 1728], P('seq', 'dp')
- out_temporal_grad: float32 [576, 1152], P('seq', 'dp')
Inputs may be any that keep to these rules, and one draw needn't show every extreme that they name: `frame_count`: some sample has 32 frames and some sample 32 // 2. patch_height * patch_width lies between 64 and 128, and equals 128 for some sample. patch_width is 32, 16 or 8.
All inputs are finite; a program needn't handle non-finite values.
Results may differ from a plain program's by a relative error of at most 0.033.
Values may be sent and summed in bfloat16 or wider, within the bound.
No kernel may reach another device: no remote copies, remote signals or barrier semaphores. Data moves between devices by JAX's collectives and lax.ppermute only.
A program may use at most 128 MiB of HBM per device.

v0:
```python
import math

import jax
import jax.numpy as jnp
from jax import lax
from jax.sharding import PartitionSpec as P

HEAD_DIM = 72


EPSILON = 1e-06
NEGATIVE = -1e30


def attend(query_rows, key_rows, value_rows, key_valid, layout, factor):
    key_layout = layout.replace("l", "m")
    logits = (
        jnp.einsum(
            layout + "," + key_layout + "->ghlm",
            query_rows,
            key_rows,
            preferred_element_type=jnp.float32,
        )
        * factor
    )
    logits = jnp.where(key_valid, logits, NEGATIVE)
    largest = jnp.max(logits, axis=-1, keepdims=True)
    powers = jnp.exp(logits - largest)
    prob_full = powers / jnp.sum(powers, axis=-1, keepdims=True)
    prob_half = prob_full.astype(jnp.bfloat16)
    output = jnp.einsum(
        "ghlm," + key_layout + "->" + layout,
        prob_half,
        value_rows,
        preferred_element_type=jnp.float32,
    )
    return (output.astype(jnp.bfloat16), prob_full, prob_half)


def attend_back(
    query_rows, key_rows, value_rows, output, out_grad, prob_full, prob_half, layout, factor
):
    key_layout = layout.replace("l", "m")
    prob_grad = jnp.einsum(
        layout + "," + key_layout + "->ghlm",
        out_grad,
        value_rows,
        preferred_element_type=jnp.float32,
    )
    row_delta = jnp.einsum(
        layout + "," + layout + "->ghl", out_grad, output, preferred_element_type=jnp.float32
    )[..., None]
    logit_grad = (prob_full * (prob_grad - row_delta)).astype(jnp.bfloat16)
    grad_query = (
        jnp.einsum(
            "ghlm," + key_layout + "->" + layout,
            logit_grad,
            key_rows,
            preferred_element_type=jnp.float32,
        )
        * factor
    )
    grad_key = (
        jnp.einsum(
            "ghlm," + layout + "->" + key_layout,
            logit_grad,
            query_rows,
            preferred_element_type=jnp.float32,
        )
        * factor
    )
    grad_value = jnp.einsum(
        "ghlm," + layout + "->" + key_layout,
        prob_half,
        out_grad,
        preferred_element_type=jnp.float32,
    )
    return (
        grad_query.astype(jnp.bfloat16),
        grad_key.astype(jnp.bfloat16),
        grad_value.astype(jnp.bfloat16),
    )


def layer_norm(mixed):
    values = mixed.astype(jnp.float32)
    centred = values - jnp.mean(values, axis=-1, keepdims=True)
    inv_std = lax.rsqrt(jnp.mean(centred * centred, axis=-1, keepdims=True) + EPSILON)
    return (centred * inv_std, inv_std)


def transposed_product(left, right):
    return jnp.einsum("rc,rd->cd", left, right, preferred_element_type=jnp.float32)


def product_by_transpose(left, right):
    return jnp.einsum("rd,cd->rc", left, right, preferred_element_type=jnp.float32)


def on_device(
    hidden,
    spatial_qkv,
    out_spatial,
    qkv_temporal,
    out_temporal,
    modulation,
    cotangent,
    frame_count,
    patch_height,
    patch_width,
):
    seq_count = lax.axis_size("seq")
    seq_place = lax.axis_index("seq")
    stream = hidden[0]
    frame_dev, slot_total, model_width = stream.shape
    frame_total = frame_dev * seq_count
    slot_dev = slot_total // seq_count
    factor = 1.0 / math.sqrt(HEAD_DIM)
    partial_value = (
        lax.all_gather(out_spatial, "seq", axis=0, tiled=True),
        lax.all_gather(qkv_temporal, "seq", axis=0, tiled=True),
        lax.all_gather(out_temporal, "seq", axis=0, tiled=True),
    )
    w_spatial, w_qkv, w_temporal = (
        lax.all_gather(partial_value[0], "dp", axis=1, tiled=True),
        lax.all_gather(partial_value[1], "dp", axis=1, tiled=True),
        lax.all_gather(partial_value[2], "dp", axis=1, tiled=True),
    )
    inner = w_spatial.shape[0]
    head_count = inner // HEAD_DIM
    frames = frame_count[0]
    slot_limit = patch_height[0] * patch_width[0]
    frame_here = seq_place * frame_dev + jnp.arange(frame_dev, dtype=jnp.int32)
    slot_ok = jnp.arange(slot_total, dtype=jnp.int32) < slot_limit
    token_mask = ((frame_here < frames)[:, None] & slot_ok[None, :]).astype(jnp.float32)[..., None]
    frame_ok = jnp.arange(frame_total, dtype=jnp.int32) < frames
    shift_vec, scale_vec, gate_vec = (modulation[0, 0], modulation[0, 1], modulation[0, 2])
    shaped = spatial_qkv[0].reshape(frame_dev, slot_total, 3, head_count, HEAD_DIM)
    query_s, key_s, value_s = (shaped[:, :, 0], shaped[:, :, 1], shaped[:, :, 2])
    out_s, full_s, half_s = attend(
        query_s, key_s, value_s, slot_ok[None, None, None, :], "glhd", factor
    )
    flat_s = out_s.reshape(-1, inner)
    branch_s = jnp.dot(flat_s, w_spatial, preferred_element_type=jnp.float32).reshape(
        frame_dev, slot_total, model_width
    )
    mixed = (stream.astype(jnp.float32) + token_mask * branch_s).astype(jnp.bfloat16)
    mixed_slots = lax.all_to_all(mixed, "seq", split_axis=1, concat_axis=0, tiled=True)
    normed, inv_std = layer_norm(mixed_slots)
    modulated = (normed * (1.0 + scale_vec) + shift_vec).astype(jnp.bfloat16)
    flat_mod = modulated.reshape(-1, model_width)
    temporal_qkv = jnp.dot(flat_mod, w_qkv, preferred_element_type=jnp.float32).astype(jnp.bfloat16)
    shaped_t = temporal_qkv.reshape(frame_total, slot_dev, 3, head_count, HEAD_DIM)
    query_t, key_t, value_t = (shaped_t[:, :, 0], shaped_t[:, :, 1], shaped_t[:, :, 2])
    out_t, full_t, half_t = attend(
        query_t, key_t, value_t, frame_ok[None, None, None, :], "lghd", factor
    )
    out_frames = lax.all_to_all(
        out_t.reshape(frame_total, slot_dev, inner), "seq", split_axis=0, concat_axis=1, tiled=True
    )
    flat_t = out_frames.reshape(-1, inner)
    branch_t = jnp.dot(flat_t, w_temporal, preferred_element_type=jnp.float32).reshape(
        frame_dev, slot_total, model_width
    )
    block_out = (mixed.astype(jnp.float32) + token_mask * gate_vec * branch_t).astype(jnp.bfloat16)
    grad_out = cotangent[0]
    branch_grad = (
        (token_mask * gate_vec * grad_out.astype(jnp.float32))
        .astype(jnp.bfloat16)
        .reshape(-1, model_width)
    )
    grad_temporal = transposed_product(flat_t, branch_grad).astype(jnp.bfloat16)
    out_t_grad = product_by_transpose(branch_grad, w_temporal).astype(jnp.bfloat16)
    out_t_grad = lax.all_to_all(
        out_t_grad.reshape(frame_dev, slot_total, inner),
        "seq",
        split_axis=1,
        concat_axis=0,
        tiled=True,
    )
    out_t_grad = out_t_grad.reshape(frame_total, slot_dev, head_count, HEAD_DIM)
    grads_t = attend_back(
        query_t, key_t, value_t, out_t, out_t_grad, full_t, half_t, "lghd", factor
    )
    qkv_t_grad = jnp.stack(grads_t, axis=2).reshape(-1, 3 * inner)
    grad_qkv = transposed_product(flat_mod, qkv_t_grad).astype(jnp.bfloat16)
    mod_grad = product_by_transpose(qkv_t_grad, w_qkv).reshape(frame_total, slot_dev, model_width)
    norm_grad = mod_grad * (1.0 + scale_vec)
    ln_grad = inv_std * (
        norm_grad
        - jnp.mean(norm_grad, axis=-1, keepdims=True)
        - normed * jnp.mean(norm_grad * normed, axis=-1, keepdims=True)
    )
    ln_frames = lax.all_to_all(
        ln_grad.astype(jnp.bfloat16), "seq", split_axis=0, concat_axis=1, tiled=True
    )
    hidden_grad = (grad_out.astype(jnp.float32) + ln_frames.astype(jnp.float32)).astype(
        jnp.bfloat16
    )
    spatial_branch_grad = (
        (token_mask * hidden_grad.astype(jnp.float32)).astype(jnp.bfloat16).reshape(-1, model_width)
    )
    grad_spatial = transposed_product(flat_s, spatial_branch_grad).astype(jnp.bfloat16)
    out_s_grad = product_by_transpose(spatial_branch_grad, w_spatial).astype(jnp.bfloat16)
    out_s_grad = out_s_grad.reshape(frame_dev, slot_total, head_count, HEAD_DIM)
    grads_s = attend_back(
        query_s, key_s, value_s, out_s, out_s_grad, full_s, half_s, "glhd", factor
    )
    qkv_s_grad = jnp.stack(grads_s, axis=2).reshape(frame_dev, slot_total, 3 * inner)
    partial_sums = (
        lax.psum_scatter(grad_spatial, "dp", scatter_dimension=1, tiled=True).astype(jnp.float32),
        lax.psum_scatter(grad_qkv, "dp", scatter_dimension=1, tiled=True).astype(jnp.float32),
        lax.psum_scatter(grad_temporal, "dp", scatter_dimension=1, tiled=True).astype(jnp.float32),
    )
    summed = (
        lax.psum_scatter(
            partial_sums[0].astype(jnp.bfloat16), "seq", scatter_dimension=0, tiled=True
        ).astype(jnp.float32),
        lax.psum_scatter(
            partial_sums[1].astype(jnp.bfloat16), "seq", scatter_dimension=0, tiled=True
        ).astype(jnp.float32),
        lax.psum_scatter(
            partial_sums[2].astype(jnp.bfloat16), "seq", scatter_dimension=0, tiled=True
        ).astype(jnp.float32),
    )
    return (block_out[None], hidden_grad[None], qkv_s_grad[None], summed[0], summed[1], summed[2])


def solution(mesh):
    placed = (
        P("dp", "seq", None, None),
        P("dp", "seq", None, None),
        P("seq", "dp"),
        P("seq", "dp"),
        P("seq", "dp"),
        P("dp", None, None),
        P("dp", "seq", None, None),
        P("dp"),
        P("dp"),
        P("dp"),
    )
    return jax.shard_map(
        on_device,
        mesh=mesh,
        in_specs=placed,
        out_specs=(
            P("dp", "seq", None, None),
            P("dp", "seq", None, None),
            P("dp", "seq", None, None),
            P("seq", "dp"),
            P("seq", "dp"),
            P("seq", "dp"),
        ),
        check_vma=False,
    )
```

profile of v0, /device:TPU:32, one launch (start us, length us, event | category | flops | bytes accessed | tf_op | source)
XLA Modules:
  0.0 675.5 jit_solution(1641682537439307269)
XLA Ops:
  7.2 13.6 %all-gather.4 = bf16[8,72,36]{1,2,0:T(8,128)(2,1)S(1)} all-gather(bf16[1,72,36]{1,2,0:T(8,128)(2,1)} %bitcast.279), channel_id=1, replica_groups=mesh['dp'=32,'seq'=8] {'seq'}, dimensions={0}, use_global_device_ids=true | all-gather | bytes 46656 | tf_op jit(solution)/shard_map/all_gather | solution.py:122
  21.7 13.0 %all-gather = bf16[8,72,36]{1,2,0:T(8,128)(2,1)S(1)} all-gather(bf16[1,72,36]{1,2,0:T(8,128)(2,1)} %bitcast.280), channel_id=1, replica_groups=mesh['dp'=32,'seq'=8] {'seq'}, dimensions={0}, use_global_device_ids=true | all-gather | bytes 46656 | tf_op jit(solution)/shard_map/all_gather | solution.py:120
  35.5 13.0 %all-gather.2 = bf16[8,144,54]{1,2,0:T(8,128)(2,1)S(1)} all-gather(bf16[1,144,54]{1,2,0:T(8,128)(2,1)} %bitcast.278), channel_id=1, replica_groups=mesh['dp'=32,'seq'=8] {'seq'}, dimensions={0}, use_global_device_ids=true | all-gather | bytes 139968 | tf_op jit(solution)/shard_map/all_gather | solution.py:121
  58.2 42.0 %all-gather.14.cloned.1.call-done = bf16[32,36,576]{2,1,0:T(8,128)(2,1)} async-done(((bf16[1,36,576]{2,1,0:T(8,128)(2,1)}), bf16[32,36,576]{2,1,0:T(8,128)(2,1)}) %all-gather.14.cloned.1.call-update) | async-done | bytes 1327120 | tf_op jit(solution)/shard_map/all_gather | solution.py:127
  107.7 4.4 all-to-all-start.2
  112.2 65.9 %all-gather.10.cloned.1.call-done = bf16[32,36,576]{2,1,0:T(8,128)(2,1)} async-done(((bf16[1,36,576]{2,1,0:T(8,128)(2,1)}), bf16[32,36,576]{2,1,0:T(8,128)(2,1)}) %all-gather.10.cloned.1.call-update) | async-done | bytes 1327120 | tf_op jit(solution)/shard_map/all_gather | solution.py:125
  187.3 4.7 all-to-all-start
  199.2 10.1 %all-to-all-done = bf16[4,128,1152]{2,0,1:T(4,128)(2,1)S(1)} async-done(((bf16[4,128,1152]{2,0,1:T(4,128)(2,1)}), bf16[4,128,1152]{2,0,1:T(4,128)(2,1)S(1)}, u32[]{:S(2)}, u32[]{:S(2)}) %all-to-all-start) | async-done | bytes 1179680 | tf_op jit(solution)/shard_map/all_to_all | solution.py:148
  214.7 45.9 %all-gather.12.cloned.1.call-done = bf16[32,54,1152]{2,1,0:T(8,128)(2,1)} async-done(((bf16[1,54,1152]{2,1,0:T(8,128)(2,1)}), bf16[32,54,1152]{2,1,0:T(8,128)(2,1)}) %all-gather.12.cloned.1.call-update) | async-done | bytes 3981328 | tf_op jit(solution)/shard_map/all_gather | solution.py:126
  260.5 5.1 reshape.267
  265.7 6.2 convolution_convert_fusion.3
  275.6 6.6 reshape.241
  285.9 5.5 fusion.64
  306.2 4.8 all-to-all-start.1
  316.2 5.7 dot_general.90
  322.0 5.1 reshape.277
  327.1 6.1 fusion.58
  334.8 4.8 all-to-all-start.3
  346.1 6.4 convolution_convert_fusion
  364.9 109.0 %fusion.59 = (bf16[576,48]{0,1:T(8,128)(2,1)S(1)}, bf16[576,48]{0,1:T(8,128)(2,1)S(1)}, bf16[1152,64]{0,1:T(8,128)(2,1)S(1)}) fusion(bf16[576,1152]{0,1:T(8,128)(2,1)S(1)} %convolution_convert_fusion.2, bf16[576,1152]{0,1:T(8,128)(2,1)} %convolution_convert_fusion.1, bf16[1152,1728]{0,1:T(8,128)(2,1)} %convolution_convert_fusion), kind=kCustom, calls=%all-reduce-scatter.3 | all-reduce-scatter fusion | flops 4128770 | bytes 6894592
  478.8 7.0 %collective-permute-start.3 = (bf16[576,48]{0,1:T(8,128)(2,1)S(1)}, bf16[576,48]{0,1:T(8,128)(2,1)S(1)}, u32[]{:S(2)}, u32[]{:S(2)}) collective-permute-start(bf16[576,48]{0,1:T(8,128)(2,1)S(1)} %get-tuple-element.16), channel_id=1, source_target_pairs={{0,32},{8,40},{16,48},{24,56},{32,64},{40,72},{48,80},{56,88},{64,... | collective-permute-start | bytes 165896
  491.0 9.9 %collective-permute-start.7 = (bf16[576,36]{0,1:T(8,128)(2,1)S(1)}, bf16[576,36]{0,1:T(8,128)(2,1)S(1)}, u32[]{:S(2)}, u32[]{:S(2)}) collective-permute-start(bf16[576,36]{0,1:T(8,128)(2,1)S(1)} %slice.42), channel_id=1, source_target_pairs={{0,64},{8,72},{16,80},{24,88},{32,96},{40,104},{48,112},{56,120},{... | collective-permute-start | bytes 124424
  502.6 4.9 collective-permute-start.20
  517.3 4.2 collective-permute-start.19
  521.6 5.4 collective-permute-start.18
  527.9 7.0 %collective-permute-start.17 = (bf16[576,48]{0,1:T(8,128)(2,1)S(1)}, bf16[576,48]{0,1:T(8,128)(2,1)}, u32[]{:S(2)}, u32[]{:S(2)}) collective-permute-start(bf16[576,48]{0,1:T(8,128)(2,1)S(1)} %get-tuple-element.17), channel_id=1, source_target_pairs={{0,40},{8,48},{16,56},{24,64},{32,72},{40,80},{48,88},{56,96},{64,... | collective-permute-start | bytes 165896
  536.9 6.4 collective-permute-start.15
  548.3 4.7 concatenate
  553.0 3.8 collective-permute-start.11
  566.7 6.6 concatenate.2
  579.9 52.9 %all-reduce.12.cloned.1.call-done = (bf16[576,36]{0,1:T(8,128)(2,1)}, bf16[576,36]{0,1:T(8,128)(2,1)}) async-done(((bf16[576,36]{0,1:T(8,128)(2,1)}, bf16[576,36]{0,1:T(8,128)(2,1)}), (bf16[576,36]{0,1:T(8,128)(2,1)}, bf16[576,36]{0,1:T(8,128)(2,1)})) %all-reduce.12.cloned.1.call-update) | async-done | bytes 82960
  635.5 31.7 %reduce-scatter.12.cloned.1.call-done = bf16[144,54]{1,0:T(8,128)(2,1)} async-done(((bf16[1152,54]{1,0:T(8,128)(2,1)}), bf16[144,54]{1,0:T(8,128)(2,1)}) %reduce-scatter.12.cloned.1.call-update) | async-done | bytes 15568
  (201 shorter events, 134.2 us)
Async XLA Ops:
  7.2 93.0 %all-gather.14.cloned.1.call-start = ((), (), s32[]{:S(2)}) async-start(), calls=%async_computation.7 | async-start | bytes 1689600 | tf_op jit(solution)/shard_map/all_gather | solution.py:127
  21.6 156.5 %all-gather.10.cloned.1.call-start = ((), (), s32[]{:S(2)}) async-start(), calls=%async_computation.5 | async-start | bytes 1689600 | tf_op jit(solution)/shard_map/all_gather | solution.py:125
  35.5 225.1 %all-gather.12.cloned.1.call-start = ((), (), s32[]{:S(2)}) async-start(), calls=%async_computation.6 | async-start | bytes 4257792 | tf_op jit(solution)/shard_map/all_gather | solution.py:126
  56.8 135.2 %copy-start.6 = (bf16[4,8,128,72]{2,3,1,0:T(8,128)(2,1)}, bf16[4,8,128,72]{2,3,1,0:T(8,128)(2,1)S(1)}, u32[]{:S(2)}) copy-start(bf16[4,8,128,72]{2,3,1,0:T(8,128)(2,1)S(1)} %convolution_convert_fusion.9) | copy-start | bytes 1769476
  107.7 79.6 %all-to-all-start.2 = ((bf16[4,128,576]{2,0,1:T(4,128)(2,1)}), bf16[4,128,576]{2,0,1:T(4,128)(2,1)S(1)}, u32[]{:S(2)}, u32[]{:S(2)}) async-start(bf16[4,128,576]{2,0,1:T(4,128)(2,1)} %copy.215), calls=%async_computation.2 | async-start | bytes 1310720 | tf_op jit(solution)/shard_map/all_to_all | solution.py:174
  187.3 22.0 %all-to-all-start = ((bf16[4,128,1152]{2,0,1:T(4,128)(2,1)}), bf16[4,128,1152]{2,0,1:T(4,128)(2,1)S(1)}, u32[]{:S(2)}, u32[]{:S(2)}) async-start(bf16[4,128,1152]{2,0,1:T(4,128)(2,1)} %copy.198), calls=%async_computation | async-start | bytes 2359296 | tf_op jit(solution)/shard_map/all_to_all | solution.py:148
  306.2 28.6 %all-to-all-start.1 = ((bf16[32,16,576]{2,1,0:T(8,128)(2,1)}), bf16[32,16,576]{2,1,0:T(8,128)(2,1)}, u32[]{:S(2)}, u32[]{:S(2)}) async-start(bf16[32,16,576]{2,1,0:T(8,128)(2,1)} %reshape.242), calls=%async_computation.1 | async-start | bytes 1310720 | tf_op jit(solution)/shard_map/all_to_all | solution.py:158
  334.8 22.3 %all-to-all-start.3 = ((bf16[32,16,1152]{2,1,0:T(8,128)(2,1)}), bf16[32,16,1152]{2,1,0:T(8,128)(2,1)}, u32[]{:S(2)}, u32[]{:S(2)}) async-start(bf16[32,16,1152]{2,1,0:T(8,128)(2,1)} %multiply_convert_fusion.2), calls=%async_computation.3 | async-start | bytes 2359296 | tf_op jit(solution)/shard_map/all_to_all | solution.py:194
  339.6 293.1 %all-reduce.12.cloned.1.call-start = ((), (), s32[]{:S(2)}) async-start(), calls=%async_computation.9 | async-start | bytes 204800
  364.9 120.9 %copy-start.9 = (bf16[1152,576]{1,0:T(8,128)(2,1)S(1)}, bf16[1152,576]{1,0:T(8,128)(2,1)}, u32[]{:S(2)}) copy-start(bf16[1152,576]{1,0:T(8,128)(2,1)} %reshape.263) | copy-start | bytes 3981316
  473.9 36.6 %collective-permute-start.6 = (bf16[576,48]{0,1:T(8,128)(2,1)S(1)}, bf16[576,48]{0,1:T(8,128)(2,1)S(1)}, u32[]{:S(2)}, u32[]{:S(2)}) collective-permute-start(bf16[576,48]{0,1:T(8,128)(2,1)S(1)} %get-tuple-element.16), channel_id=1, source_target_pairs={{0,56},{8,64},{16,72},{24,80},{32,88},{40,96},{48,104},{56,112},{6... | collective-permute-start | bytes 165896
  475.2 38.7 %collective-permute-start.5 = (bf16[576,48]{0,1:T(8,128)(2,1)S(1)}, bf16[576,48]{0,1:T(8,128)(2,1)S(1)}, u32[]{:S(2)}, u32[]{:S(2)}) collective-permute-start(bf16[576,48]{0,1:T(8,128)(2,1)S(1)} %get-tuple-element.16), channel_id=1, source_target_pairs={{0,48},{8,56},{16,64},{24,72},{32,80},{40,88},{48,96},{56,104},{64... | collective-permute-start | bytes 165896
  476.5 40.8 %collective-permute-start.4 = (bf16[576,48]{0,1:T(8,128)(2,1)S(1)}, bf16[576,48]{0,1:T(8,128)(2,1)S(1)}, u32[]{:S(2)}, u32[]{:S(2)}) collective-permute-start(bf16[576,48]{0,1:T(8,128)(2,1)S(1)} %get-tuple-element.16), channel_id=1, source_target_pairs={{0,40},{8,48},{16,56},{24,64},{32,72},{40,80},{48,88},{56,96},{64,... | collective-permute-start | bytes 165896
  478.8 42.8 %collective-permute-start.3 = (bf16[576,48]{0,1:T(8,128)(2,1)S(1)}, bf16[576,48]{0,1:T(8,128)(2,1)S(1)}, u32[]{:S(2)}, u32[]{:S(2)}) collective-permute-start(bf16[576,48]{0,1:T(8,128)(2,1)S(1)} %get-tuple-element.16), channel_id=1, source_target_pairs={{0,32},{8,40},{16,48},{24,56},{32,64},{40,72},{48,80},{56,88},{64,... | collective-permute-start | bytes 165896
  491.0 11.7 %collective-permute-start.7 = (bf16[576,36]{0,1:T(8,128)(2,1)S(1)}, bf16[576,36]{0,1:T(8,128)(2,1)S(1)}, u32[]{:S(2)}, u32[]{:S(2)}) collective-permute-start(bf16[576,36]{0,1:T(8,128)(2,1)S(1)} %slice.42), channel_id=1, source_target_pairs={{0,64},{8,72},{16,80},{24,88},{32,96},{40,104},{48,112},{56,120},{... | collective-permute-start | bytes 124424
  502.6 6.7 collective-permute-start.20
  509.3 18.6 %collective-permute-start.2 = (bf16[576,48]{0,1:T(8,128)(2,1)S(1)}, bf16[576,48]{0,1:T(8,128)(2,1)S(1)}, u32[]{:S(2)}, u32[]{:S(2)}) collective-permute-start(bf16[576,48]{0,1:T(8,128)(2,1)S(1)} %get-tuple-element.16), channel_id=1, source_target_pairs={{0,24},{8,32},{16,40},{24,48},{32,56},{40,64},{48,72},{56,80},{64,... | collective-permute-start | bytes 165896
  510.6 24.3 %collective-permute-start.1 = (bf16[576,48]{0,1:T(8,128)(2,1)S(1)}, bf16[576,48]{0,1:T(8,128)(2,1)S(1)}, u32[]{:S(2)}, u32[]{:S(2)}) collective-permute-start(bf16[576,48]{0,1:T(8,128)(2,1)S(1)} %get-tuple-element.16), channel_id=1, source_target_pairs={{0,16},{8,24},{16,32},{24,40},{32,48},{40,56},{48,64},{56,72},{64,... | collective-permute-start | bytes 165896
  513.9 22.9 %collective-permute-start = (bf16[576,48]{0,1:T(8,128)(2,1)S(1)}, bf16[576,48]{0,1:T(8,128)(2,1)S(1)}, u32[]{:S(2)}, u32[]{:S(2)}) collective-permute-start(bf16[576,48]{0,1:T(8,128)(2,1)S(1)} %get-tuple-element.16), channel_id=1, source_target_pairs={{0,8},{8,16},{16,24},{24,32},{32,40},{40,48},{48,56},{56,64},{64,7... | collective-permute-start | bytes 165896
  517.3 25.9 %collective-permute-start.19 = (bf16[576,48]{0,1:T(8,128)(2,1)S(1)}, bf16[576,48]{0,1:T(8,128)(2,1)S(1)}, u32[]{:S(2)}, u32[]{:S(2)}) collective-permute-start(bf16[576,48]{0,1:T(8,128)(2,1)S(1)} %get-tuple-element.17), channel_id=1, source_target_pairs={{0,56},{8,64},{16,72},{24,80},{32,88},{40,96},{48,104},{56,112},{6... | collective-permute-start | bytes 165896
  521.6 23.6 %collective-permute-start.18 = (bf16[576,48]{0,1:T(8,128)(2,1)S(1)}, bf16[576,48]{0,1:T(8,128)(2,1)S(1)}, u32[]{:S(2)}, u32[]{:S(2)}) collective-permute-start(bf16[576,48]{0,1:T(8,128)(2,1)S(1)} %get-tuple-element.17), channel_id=1, source_target_pairs={{0,48},{8,56},{16,64},{24,72},{32,80},{40,88},{48,96},{56,104},{64... | collective-permute-start | bytes 165896
  527.9 25.1 %collective-permute-start.17 = (bf16[576,48]{0,1:T(8,128)(2,1)S(1)}, bf16[576,48]{0,1:T(8,128)(2,1)}, u32[]{:S(2)}, u32[]{:S(2)}) collective-permute-start(bf16[576,48]{0,1:T(8,128)(2,1)S(1)} %get-tuple-element.17), channel_id=1, source_target_pairs={{0,40},{8,48},{16,56},{24,64},{32,72},{40,80},{48,88},{56,96},{64,... | collective-permute-start | bytes 165896
  534.9 22.0 %collective-permute-start.16 = (bf16[576,48]{0,1:T(8,128)(2,1)S(1)}, bf16[576,48]{0,1:T(8,128)(2,1)}, u32[]{:S(2)}, u32[]{:S(2)}) collective-permute-start(bf16[576,48]{0,1:T(8,128)(2,1)S(1)} %get-tuple-element.17), channel_id=1, source_target_pairs={{0,32},{8,40},{16,48},{24,56},{32,64},{40,72},{48,80},{56,88},{64,... | collective-permute-start | bytes 165896
  536.9 22.5 %collective-permute-start.15 = (bf16[576,48]{0,1:T(8,128)(2,1)S(1)}, bf16[576,48]{0,1:T(8,128)(2,1)}, u32[]{:S(2)}, u32[]{:S(2)}) collective-permute-start(bf16[576,48]{0,1:T(8,128)(2,1)S(1)} %get-tuple-element.17), channel_id=1, source_target_pairs={{0,24},{8,32},{16,40},{24,48},{32,56},{40,64},{48,72},{56,80},{64,... | collective-permute-start | bytes 165896
  543.3 18.9 %collective-permute-start.14 = (bf16[576,48]{0,1:T(8,128)(2,1)S(1)}, bf16[576,48]{0,1:T(8,128)(2,1)}, u32[]{:S(2)}, u32[]{:S(2)}) collective-permute-start(bf16[576,48]{0,1:T(8,128)(2,1)S(1)} %get-tuple-element.17), channel_id=1, source_target_pairs={{0,16},{8,24},{16,32},{24,40},{32,48},{40,56},{48,64},{56,72},{64,... | collective-permute-start | bytes 165896
  545.8 18.9 %collective-permute-start.13 = (bf16[576,48]{0,1:T(8,128)(2,1)S(1)}, bf16[576,48]{0,1:T(8,128)(2,1)}, u32[]{:S(2)}, u32[]{:S(2)}) collective-permute-start(bf16[576,48]{0,1:T(8,128)(2,1)S(1)} %get-tuple-element.17), channel_id=1, source_target_pairs={{0,8},{8,16},{16,24},{24,32},{32,40},{40,48},{48,56},{56,64},{64,7... | collective-permute-start | bytes 165896
  553.0 21.0 %collective-permute-start.11 = (bf16[1152,64]{0,1:T(8,128)(2,1)S(1)}, bf16[1152,64]{0,1:T(8,128)(2,1)S(1)}, u32[]{:S(2)}, u32[]{:S(2)}) collective-permute-start(bf16[1152,64]{0,1:T(8,128)(2,1)S(1)} %get-tuple-element.18), channel_id=1, source_target_pairs={{0,32},{8,40},{16,48},{24,56},{32,64},{40,72},{48,80},{56,88},{64,... | collective-permute-start | bytes 442376
  556.9 17.2 %collective-permute-start.10 = (bf16[1152,64]{0,1:T(8,128)(2,1)S(1)}, bf16[1152,64]{0,1:T(8,128)(2,1)S(1)}, u32[]{:S(2)}, u32[]{:S(2)}) collective-permute-start(bf16[1152,64]{0,1:T(8,128)(2,1)S(1)} %get-tuple-element.18), channel_id=1, source_target_pairs={{0,24},{8,32},{16,40},{24,48},{32,56},{40,64},{48,72},{56,80},{64,... | collective-permute-start | bytes 442376
  559.4 14.7 %collective-permute-start.9 = (bf16[1152,64]{0,1:T(8,128)(2,1)S(1)}, bf16[1152,64]{0,1:T(8,128)(2,1)S(1)}, u32[]{:S(2)}, u32[]{:S(2)}) collective-permute-start(bf16[1152,64]{0,1:T(8,128)(2,1)S(1)} %get-tuple-element.18), channel_id=1, source_target_pairs={{0,16},{8,24},{16,32},{24,40},{32,48},{40,56},{48,64},{56,72},{64,... | collective-permute-start | bytes 442376
  562.2 12.5 %collective-permute-start.8 = (bf16[1152,64]{0,1:T(8,128)(2,1)S(1)}, bf16[1152,64]{0,1:T(8,128)(2,1)S(1)}, u32[]{:S(2)}, u32[]{:S(2)}) collective-permute-start(bf16[1152,64]{0,1:T(8,128)(2,1)S(1)} %get-tuple-element.18), channel_id=1, source_target_pairs={{0,8},{8,16},{16,24},{24,32},{32,40},{40,48},{48,56},{56,64},{64,7... | collective-permute-start | bytes 442376
  564.7 9.3 %collective-permute-start.12 = (bf16[1152,54]{0,1:T(8,128)(2,1)S(1)}, bf16[1152,54]{0,1:T(8,128)(2,1)S(1)}, u32[]{:S(2)}, u32[]{:S(2)}) collective-permute-start(bf16[1152,54]{0,1:T(8,128)(2,1)S(1)} %slice.43), channel_id=1, source_target_pairs={{0,40},{8,48},{16,56},{24,64},{32,72},{40,80},{48,88},{56,96},{64,... | collective-permute-start | bytes 373256
  574.0 93.3 %reduce-scatter.12.cloned.1.call-start = ((), (), s32[]{:S(2)}) async-start(), calls=%async_computation.8 | async-start | bytes 331776
  (32 other events, 312.5 us)
Sparse Core Ops, SparseCore 0:
  21.8 78.3 all-gather.13
  103.4 74.7 all-gather.9
  180.8 79.7 all-gather.11
  574.1 58.5 all-reduce.11
  635.2 31.9 reduce-scatter.11
where the time goes:
time: 685 us; the launch traced here: 676 us
  waiting for transfers between devices  250 us (36%)
  blocking collectives  149 us (22%)
  starting transfers between devices  95.3 us (14%)
  local copies, waits for them, and re-layouts  85.7 us (13%)
  matrix products  56.3 us (8%)
  other arithmetic  20.7 us (3%)
  between operations  18.7 us (3%)
    unnamed x1, blocking collectives  109 us
    unnamed x28, waiting for transfers between devices  85.8 us
    unnamed x23, starting transfers between devices  76.5 us
    all_gather x1, waiting for transfers between devices, on_device(): lax.all_gather(partial_value[0], 'dp', axis=1, tiled=True)  65.9 us
    all_gather x1, waiting for transfers between devices, on_device(): lax.all_gather(partial_value[1], 'dp', axis=1, tiled=True)  45.9 us
    unnamed x88, local copies, waits for them, and re-layouts  42.4 us
    all_gather x1, waiting for transfers between devices, on_device(): lax.all_gather(partial_value[2], 'dp', axis=1, tiled=True)  42 us
  transfers between devices with their start and end apart: 30, of which 8 were waited for; matrix products, arithmetic and copies ran while one was open for 15% of the time, Pallas kernels for 0%

commit v1 on v0

v1 whole, which is shorter than its diff:
```python
import math

import jax
import jax.numpy as jnp
from jax import lax
from jax.sharding import Mesh
from jax.sharding import PartitionSpec as P

HEAD_DIM = 72


EPSILON = 1e-06
NEGATIVE = -1e30


def attend(query_rows, key_rows, value_rows, key_valid, layout, factor):
    key_layout = layout.replace("l", "m")
    logits = (
        jnp.einsum(
            layout + "," + key_layout + "->ghlm",
            query_rows,
            key_rows,
            preferred_element_type=jnp.float32,
        )
        * factor
    )
    logits = jnp.where(key_valid, logits, NEGATIVE)
    largest = jnp.max(logits, axis=-1, keepdims=True)
    powers = jnp.exp(logits - largest)
    prob_full = powers / jnp.sum(powers, axis=-1, keepdims=True)
    prob_half = prob_full.astype(jnp.bfloat16)
    output = jnp.einsum(
        "ghlm," + key_layout + "->" + layout,
        prob_half,
        value_rows,
        preferred_element_type=jnp.float32,
    )
    return (output.astype(jnp.bfloat16), prob_full, prob_half)


def attend_back(
    query_rows, key_rows, value_rows, output, out_grad, prob_full, prob_half, layout, factor
):
    key_layout = layout.replace("l", "m")
    prob_grad = jnp.einsum(
        layout + "," + key_layout + "->ghlm",
        out_grad,
        value_rows,
        preferred_element_type=jnp.float32,
    )
    row_delta = jnp.einsum(
        layout + "," + layout + "->ghl", out_grad, output, preferred_element_type=jnp.float32
    )[..., None]
    logit_grad = (prob_full * (prob_grad - row_delta)).astype(jnp.bfloat16)
    grad_query = (
        jnp.einsum(
            "ghlm," + key_layout + "->" + layout,
            logit_grad,
            key_rows,
            preferred_element_type=jnp.float32,
        )
        * factor
    )
    grad_key = (
        jnp.einsum(
            "ghlm," + layout + "->" + key_layout,
            logit_grad,
            query_rows,
            preferred_element_type=jnp.float32,
        )
        * factor
    )
    grad_value = jnp.einsum(
        "ghlm," + layout + "->" + key_layout,
        prob_half,
        out_grad,
        preferred_element_type=jnp.float32,
    )
    return (
        grad_query.astype(jnp.bfloat16),
        grad_key.astype(jnp.bfloat16),
        grad_value.astype(jnp.bfloat16),
    )


def layer_norm(mixed):
    values = mixed.astype(jnp.float32)
    centred = values - jnp.mean(values, axis=-1, keepdims=True)
    inv_std = lax.rsqrt(jnp.mean(centred * centred, axis=-1, keepdims=True) + EPSILON)
    return (centred * inv_std, inv_std)


def transposed_product(left, right):
    return jnp.einsum("rc,rd->cd", left, right, preferred_element_type=jnp.float32)


def product_by_transpose(left, right):
    return jnp.einsum("rd,cd->rc", left, right, preferred_element_type=jnp.float32)


def weight_rows(out_spatial, qkv_temporal, out_temporal):
    packed = jnp.concatenate(
        [jnp.concatenate([out_spatial.T, out_temporal.T], axis=1), qkv_temporal.T], axis=0
    )
    near = lax.all_gather(packed, ("y", "c"), axis=0, tiled=False)
    narrow = out_spatial.shape[1]
    half = out_spatial.shape[0]
    pair = jnp.transpose(near[:, :narrow], (1, 0, 2))
    first = pair[:, :, :half].reshape(narrow, -1)
    second = pair[:, :, half:].reshape(narrow, -1)
    wide = jnp.transpose(near[:, narrow:], (1, 0, 2)).reshape(near.shape[1] - narrow, -1)
    rows = jnp.concatenate([jnp.concatenate([first, second], axis=1), wide], axis=0)
    far = lax.all_gather(rows, ("x", "z"), axis=0, tiled=False)
    inner = first.shape[1]
    w_pair = far[:, :narrow].reshape(-1, 2 * inner)
    w_wide = far[:, narrow:].reshape(-1, far.shape[2])
    return (w_pair[:, :inner], w_wide, w_pair[:, inner:])


def exchange(rows, axes):
    return lax.all_to_all(rows, axes, 0, 0, tiled=True)


def halve_and_quarter(terms):
    split = terms.reshape((4, 2) + terms.shape[1:])
    split = jnp.transpose(split, (1, 0, 2, 3))
    pairs = exchange(split, "c").astype(jnp.float32)
    pairs = (pairs[0] + pairs[1]).astype(jnp.bfloat16)
    quads = exchange(pairs, "y").astype(jnp.float32)
    return ((quads[0] + quads[1]) + (quads[2] + quads[3])).astype(jnp.bfloat16)


def on_device(
    hidden,
    spatial_qkv,
    out_spatial,
    qkv_temporal,
    out_temporal,
    modulation,
    cotangent,
    frame_count,
    patch_height,
    patch_width,
):
    seq_count = lax.axis_size(("y", "c"))
    seq_place = lax.axis_index(("y", "c"))
    stream = hidden[0]
    grad_out = cotangent[0]
    frame_dev, slot_total, model_width = stream.shape
    frame_total = frame_dev * seq_count
    slot_dev = slot_total // seq_count
    factor = 1.0 / math.sqrt(HEAD_DIM)

    def to_slots(rows):
        width = rows.shape[-1]
        split = rows.reshape(frame_dev, seq_count, slot_dev, width)
        moved = exchange(jnp.transpose(split, (1, 0, 2, 3)), ("y", "c"))
        return moved.reshape(frame_total, slot_dev, width)

    def to_frames(rows):
        width = rows.shape[-1]
        split = rows.reshape(seq_count, frame_dev, slot_dev, width)
        moved = jnp.transpose(exchange(split, ("y", "c")), (1, 0, 2, 3))
        return moved.reshape(frame_dev, slot_total, width)

    w_spatial, w_qkv, w_temporal = weight_rows(out_spatial, qkv_temporal, out_temporal)
    inner = w_spatial.shape[1]
    head_count = inner // HEAD_DIM
    frames = frame_count[0]
    slot_limit = patch_height[0] * patch_width[0]
    frame_here = seq_place * frame_dev + jnp.arange(frame_dev, dtype=jnp.int32)
    slot_here = seq_place * slot_dev + jnp.arange(slot_dev, dtype=jnp.int32)
    slot_ok = jnp.arange(slot_total, dtype=jnp.int32) < slot_limit
    frame_ok = jnp.arange(frame_total, dtype=jnp.int32) < frames
    mask_f = ((frame_here < frames)[:, None] & slot_ok[None, :]).astype(jnp.float32)[..., None]
    mask_s = (frame_ok[:, None] & (slot_here < slot_limit)[None, :]).astype(jnp.float32)[..., None]
    shift_vec, scale_vec, gate_vec = (modulation[0, 0], modulation[0, 1], modulation[0, 2])

    stream_s = to_slots(stream)
    grad_out_s = to_slots(grad_out)
    shaped = spatial_qkv[0].reshape(frame_dev, slot_total, 3, head_count, HEAD_DIM)
    query_s, key_s, value_s = (shaped[:, :, 0], shaped[:, :, 1], shaped[:, :, 2])
    out_s, full_s, half_s = attend(
        query_s, key_s, value_s, slot_ok[None, None, None, :], "glhd", factor
    )
    rows_s = out_s.reshape(frame_dev, slot_total, inner)
    flat_s = to_slots(rows_s).reshape(-1, inner)

    branch_s = product_by_transpose(flat_s, w_spatial).reshape(frame_total, slot_dev, model_width)
    mixed_s = (stream_s.astype(jnp.float32) + mask_s * branch_s).astype(jnp.bfloat16)
    normed, inv_std = layer_norm(mixed_s)
    modulated = (normed * (1.0 + scale_vec) + shift_vec).astype(jnp.bfloat16)
    flat_mod = modulated.reshape(-1, model_width)
    temporal_qkv = product_by_transpose(flat_mod, w_qkv).astype(jnp.bfloat16)
    shaped_t = temporal_qkv.reshape(frame_total, slot_dev, 3, head_count, HEAD_DIM)
    query_t, key_t, value_t = (shaped_t[:, :, 0], shaped_t[:, :, 1], shaped_t[:, :, 2])
    out_t, full_t, half_t = attend(
        query_t, key_t, value_t, frame_ok[None, None, None, :], "lghd", factor
    )
    rows_t = out_t.reshape(frame_total, slot_dev, inner)
    flat_t = rows_t.reshape(-1, inner)

    branch_grad = (
        (mask_s * gate_vec * grad_out_s.astype(jnp.float32))
        .astype(jnp.bfloat16)
        .reshape(-1, model_width)
    )
    grad_temporal = transposed_product(flat_t, branch_grad).astype(jnp.bfloat16)
    out_t_grad = jnp.dot(branch_grad, w_temporal, preferred_element_type=jnp.float32)
    out_t_grad = out_t_grad.astype(jnp.bfloat16).reshape(
        frame_total, slot_dev, head_count, HEAD_DIM
    )
    grads_t = attend_back(
        query_t, key_t, value_t, out_t, out_t_grad, full_t, half_t, "lghd", factor
    )
    qkv_t_grad = jnp.stack(grads_t, axis=2).reshape(-1, 3 * inner)
    grad_qkv = transposed_product(flat_mod, qkv_t_grad).astype(jnp.bfloat16)
    mod_grad = jnp.dot(qkv_t_grad, w_qkv, preferred_element_type=jnp.float32)
    norm_grad = mod_grad.reshape(frame_total, slot_dev, model_width) * (1.0 + scale_vec)
    ln_grad = inv_std * (
        norm_grad
        - jnp.mean(norm_grad, axis=-1, keepdims=True)
        - normed * jnp.mean(norm_grad * normed, axis=-1, keepdims=True)
    )
    ln_grad = ln_grad.astype(jnp.bfloat16)
    hidden_grad_s = (grad_out_s.astype(jnp.float32) + ln_grad.astype(jnp.float32)).astype(
        jnp.bfloat16
    )
    branch_grad_s = (
        (mask_s * hidden_grad_s.astype(jnp.float32)).astype(jnp.bfloat16).reshape(-1, model_width)
    )
    grad_spatial = transposed_product(flat_s, branch_grad_s).astype(jnp.bfloat16)
    ln_frames = to_frames(ln_grad)

    sum_qkv = halve_and_quarter(grad_qkv.reshape(seq_count, -1, 3 * inner))
    grad_pair = jnp.concatenate(
        [grad_spatial.reshape(seq_count, -1, model_width), grad_temporal.reshape(seq_count, -1, model_width)],
        axis=1,
    )
    sum_pair = halve_and_quarter(grad_pair)
    dp_count = lax.axis_size(("x", "z"))
    chunks = jnp.concatenate(
        [
            sum_pair.T.reshape(dp_count, -1, sum_pair.shape[0]),
            sum_qkv.T.reshape(dp_count, -1, sum_qkv.shape[0]),
        ],
        axis=1,
    )
    total = jnp.sum(exchange(chunks, ("x", "z")).astype(jnp.float32), axis=0)
    narrow = out_spatial.shape[1]
    half = out_spatial.shape[0]
    summed = (total[:narrow, :half].T, total[narrow:].T, total[:narrow, half:].T)

    frames_t = to_frames(rows_t).reshape(-1, inner)
    branch_t = product_by_transpose(frames_t, w_temporal).reshape(
        frame_dev, slot_total, model_width
    )
    branch_f = product_by_transpose(rows_s.reshape(-1, inner), w_spatial).reshape(
        frame_dev, slot_total, model_width
    )
    mixed = (stream.astype(jnp.float32) + mask_f * branch_f).astype(jnp.bfloat16)
    block_out = (mixed.astype(jnp.float32) + mask_f * gate_vec * branch_t).astype(jnp.bfloat16)
    hidden_grad = (grad_out.astype(jnp.float32) + ln_frames.astype(jnp.float32)).astype(
        jnp.bfloat16
    )
    spatial_branch_grad = (
        (mask_f * hidden_grad.astype(jnp.float32)).astype(jnp.bfloat16).reshape(-1, model_width)
    )
    out_s_grad = jnp.dot(spatial_branch_grad, w_spatial, preferred_element_type=jnp.float32)
    out_s_grad = out_s_grad.astype(jnp.bfloat16).reshape(
        frame_dev, slot_total, head_count, HEAD_DIM
    )
    grads_s = attend_back(
        query_s, key_s, value_s, out_s, out_s_grad, full_s, half_s, "glhd", factor
    )
    qkv_s_grad = jnp.stack(grads_s, axis=2).reshape(frame_dev, slot_total, 3 * inner)
    return (block_out[None], hidden_grad[None], qkv_s_grad[None], summed[0], summed[1], summed[2])


def solution(mesh):
    torus = Mesh(mesh.devices.reshape(4, 8, 4, 2), ("x", "z", "y", "c"))
    dp, seq = ("x", "z"), ("y", "c")
    tokens = P(dp, seq, None, None)
    weight = P(seq, dp)
    placed = (
        tokens,
        tokens,
        weight,
        weight,
        weight,
        P(dp, None, None),
        tokens,
        P(dp),
        P(dp),
        P(dp),
    )
    return jax.shard_map(
        on_device,
        mesh=torus,
        in_specs=placed,
        out_specs=(tokens, tokens, tokens, weight, weight, weight),
        check_vma=False,
    )
```

time: 685 us -> 394 us (0.58)
  blocking collectives: 149 us -> 13.4 us
  waiting for transfers between devices: 250 us -> 135 us
  starting transfers between devices: 95.3 us -> 45.6 us
  other arithmetic: 20.7 us -> 34.8 us
    all_gather x3 -> x1, waiting for transfers between devices: 154 us -> 40.6 us  [weight_rows(): far = lax.all_gather(rows, ('x', 'z'), axis=0, tiled=False)]
    unnamed x1 -> x0, blocking collectives: 109 us -> none
    unnamed x28 -> x1, waiting for transfers between devices: 85.8 us -> 0.02 us
    all_to_all x4 -> x10, waiting for transfers between devices: 10.5 us -> 94.2 us  [exchange(): return lax.all_to_all(rows, axes, 0, 0, tiled=True)]
    unnamed x23 -> x0, starting transfers between devices: 76.5 us -> none
    unnamed x88 -> x66, local copies, waits for them, and re-layouts: 42.4 us -> 10.2 us
    all_to_all x4 -> x10, starting transfers between devices: 18.7 us -> 45.6 us  [exchange(): return lax.all_to_all(rows, axes, 0, 0, tiled=True)]
    all_gather x3 -> x1, blocking collectives: 39.6 us -> 13.4 us  [weight_rows(): near = lax.all_gather(packed, ('y', 'c'), axis=0, tiled=False)]
  transfers between devices with their start and end apart: 30 -> 11, of which waited for: 8 -> 9; matrix products, arithmetic and copies ran while one was open for 15% -> 18% of each run, Pallas kernels for 0% -> 0%
where the time goes in v1:
time: 394 us; the launch traced here: 388 us
  waiting for transfers between devices  135 us (34%)
  local copies, waits for them, and re-layouts  89.2 us (23%)
  matrix products  53.4 us (14%)
  starting transfers between devices  45.6 us (12%)
  other arithmetic  34.8 us (9%)
  between operations  16.8 us (4%)
  blocking collectives  13.4 us (3%)
    all_to_all x10, waiting for transfers between devices, exchange(): return lax.all_to_all(rows, axes, 0, 0, tiled=True)  94.2 us
    all_to_all x10, starting transfers between devices, exchange(): return lax.all_to_all(rows, axes, 0, 0, tiled=True)  45.6 us
    all_gather x1, waiting for transfers between devices, weight_rows(): far = lax.all_gather(rows, ('x', 'z'), axis=0, tiled=False)  40.6 us
    all_gather x1, blocking collectives, weight_rows(): near = lax.all_gather(packed, ('y', 'c'), axis=0, tiled=False)  13.4 us
    dot_general x4, matrix products, product_by_transpose(): jnp.einsum('rd,cd->rc', left, right, preferred_element_type=jnp.float32)  13 us
    unnamed x66, local copies, waits for them, and re-layouts  10.2 us
    reshape x2, local copies, waits for them, and re-layouts, weight_rows(): w_wide = far[:, narrow:].reshape(-1, far.shape[2])  10.1 us
    dot_general x3, matrix products, transposed_product(): jnp.einsum('rc,rd->cd', left, right, preferred_element_type=jnp.float32)  8.25 us
  transfers between devices with their start and end apart: 11, of which 9 were waited for; matrix products, arithmetic and copies ran while one was open for 18% of the time, Pallas kernels for 0%

profile of v1, /device:TPU:32, one launch (start us, length us, event | category | flops | bytes accessed | tf_op | source)
XLA Modules:
  0.0 388.1 jit_solution(7983256133743017301)
XLA Ops:
  9.9 13.4 %all-gather.2 = bf16[8,90,144]{1,2,0:T(8,128)(2,1)S(1)} all-gather(bf16[1,90,144]{1,2,0:T(8,128)(2,1)S(1)} %maximum_bitcast_fusion), channel_id=2, replica_groups=mesh['x'=4,'z'=8,'y'=4,'c'=2] {'y','c'}, dimensions={0}, use_global_device_ids=true | all-gather | bytes 233280 | tf_op jit(solution)/shard_map/all_gather | solution.py:105
  33.8 3.8 all-to-all-start.1
  39.3 10.0 %all-to-all-done.1 = bf16[8,4,16,576]{3,2,1,0:T(8,128)(2,1)S(1)} async-done(((bf16[8,4,16,576]{3,2,1,0:T(8,128)(2,1)}), bf16[8,4,16,576]{3,2,1,0:T(8,128)(2,1)S(1)}, u32[]{:S(2)}, u32[]{:S(2)}) %all-to-all-start.1) | async-done | bytes 589856 | tf_op jit(solution)/shard_map/all_to_all | solution.py:121
  49.3 3.7 all-to-all-start.3
  54.6 15.6 %all-to-all-done.3 = bf16[8,4,16,1152]{3,2,1,0:T(8,128)(2,1)S(1)} async-done(((bf16[8,4,16,1152]{3,2,1,0:T(8,128)(2,1)}), bf16[8,4,16,1152]{3,2,1,0:T(8,128)(2,1)S(1)}, u32[]{:S(2)}, u32[]{:S(2)}) %all-to-all-start.3) | async-done | bytes 1179680 | tf_op jit(solution)/shard_map/all_to_all | solution.py:121
  70.3 4.7 %all-to-all-start = ((bf16[8,4,16,1152]{3,2,1,0:T(8,128)(2,1)}), bf16[8,4,16,1152]{3,2,1,0:T(8,128)(2,1)}, u32[]{:S(2)}, u32[]{:S(2)}) async-start(bf16[8,4,16,1152]{3,2,1,0:T(8,128)(2,1)} %bitcast.245), calls=%async_computation | async-start | bytes 2359296 | tf_op jit(solution)/shard_map/all_to_all | solution.py:121
  77.8 40.6 %all-gather.6.cloned.1.call-done = bf16[32,90,1152]{2,1,0:T(8,128)(2,1)} async-done(((bf16[1,90,1152]{2,1,0:T(8,128)(2,1)}), bf16[32,90,1152]{2,1,0:T(8,128)(2,1)}) %all-gather.6.cloned.1.call-update) | async-done | bytes 6635536 | tf_op jit(solution)/shard_map/all_gather | solution.py:113
  126.0 7.1 %slice.137 = bf16[32,54,1152]{2,1,0:T(8,128)(2,1)} slice(bf16[32,90,1152]{2,1,0:T(8,128)(2,1)} %all-gather.6.cloned.1.call-done), slice={[0:32], [36:90], [0:1152]} | slice | bytes 7962624 | tf_op jit(solution)/shard_map/slice | solution.py:116
  133.1 5.0 %reshape.261 = bf16[1728,1152]{1,0:T(8,128)(2,1)} reshape(bf16[32,54,1152]{2,1,0:T(8,128)(2,1)} %slice.137) | data formatting | bytes 7962624 | tf_op jit(solution)/shard_map/reshape | solution.py:116
  139.6 4.6 %convolution_convert_fusion.3 = bf16[512,1728]{0,1:T(8,128)(2,1)S(1)} fusion(bf16[512,1152]{1,0:T(8,128)(2,1)S(1)} %bitcast.260, bf16[1728,1152]{1,0:T(8,128)(2,1)} %reshape.261), kind=kOutput, calls=%fused_computation.15 | convolution fusion | flops 2039316480 | bytes 6930432 | tf_op jit(solution)/shard_map/rd,cd->rc/dot_general | solution.py:98
  146.8 5.1 %reshape.262 = bf16[32,16,3,8,72]{4,3,2,1,0:T(8,128)(2,1)S(1)} reshape(bf16[512,1728]{1,0:T(8,128)(2,1)} %copy.93) | data formatting | bytes 3538944 | tf_op jit(solution)/shard_map/reshape | solution.py:195
  165.1 5.4 %multiply_reduce_fusion.2 = (f32[16,8,32]{2,1,0:T(8,128)S(1)}, bf16[16,8,72,32]{2,3,1,0:T(8,128)(2,1)}) fusion(f32[16,8,32,72]{3,1,0,2:T(8,128)} %bitcast_convert_fusion, f32[16,8,32,32]{2,3,1,0:T(8,128)} %get-tuple-element.31, f32[16,8,32]{2,1,0:T(8,128)S(1)} %get-tuple-element.30, bf16[32,16,1,8,72]{4,3,2,1,0:T(8,128)(2,1)} %get-tuple-element.21), kind=kOutput, calls=%fused_computation.43 | convolution fusion | flops 20312064 | bytes 2916352 | tf_op jit(solution)/shard_map/ghlm,mghd->lghd/dot_general | solution.py:32
  175.9 5.1 %reshape.290 = bf16[1728,1152,1]{1,0,2:T(8,128)(2,1)} reshape(bf16[32,54,1152]{2,1,0:T(8,128)(2,1)} %slice.137) | data formatting | bytes 7962624 | tf_op jit(solution)/shard_map/reshape | solution.py:116
  194.8 5.5 %fusion.69 = (f32[32,16]{1,0:T(8,128)S(1)}, f32[32,16]{1,0:T(8,128)S(1)}, f32[32,16,1152]{2,1,0:T(8,128)S(1)}) fusion(f32[32,16]{1,0:T(8,128)S(1)} %add_rsqrt_fusion, f32[32,16,1152]{2,1,0:T(8,128)S(1)} %copy-done.1, f32[32,16]{1,0:T(8,128)S(1)} %broadcast_multiply_fusion.2, f32[1152]{0:T(1024)S(1)} %get-tuple-element.16, ...), kind=kOutput, calls=%fused_computation.151 | convolution fusion | flops 2041969664 | bytes 10482176 | tf_op jit(solution)/shard_map/dot_general | solution.py:218
  206.4 3.9 all-to-all-start.5
  210.3 6.3 %convolution_convert_fusion = bf16[1152,1728]{0,1:T(8,128)(2,1)} fusion(bf16[512,1152]{1,0:T(8,128)(2,1)} %bitcast.261, bf16[512,1728]{1,0:T(8,128)(2,1)} %reshape.268), kind=kOutput, calls=%fused_computation.2 | convolution fusion | flops 2040422400 | bytes 6930432 | tf_op jit(solution)/shard_map/rc,rd->cd/dot_general | solution.py:94
  216.6 6.4 %copy.122 = bf16[1152,1728]{1,0:T(8,128)(2,1)} copy(bf16[1152,1728]{0,1:T(8,128)(2,1)} %convolution_convert_fusion) | data formatting | bytes 7962624 | tf_op jit(solution)/shard_map/convert_element_type | solution.py:217
  223.1 4.5 %copy.123 = bf16[2,4,144,1728]{3,2,1,0:T(8,128)(2,1)} copy(bf16[2,4,144,1728]{3,2,0,1:T(8,128)(2,1)} %bitcast.249) | data formatting | bytes 7962624 | tf_op jit(solution)/shard_map/transpose | solution.py:126
  227.5 5.6 %all-to-all-start.7 = ((bf16[2,4,144,1728]{3,2,1,0:T(8,128)(2,1)}), bf16[2,4,144,1728]{3,2,1,0:T(8,128)(2,1)}, u32[]{:S(2)}, u32[]{:S(2)}) async-start(bf16[2,4,144,1728]{3,2,1,0:T(8,128)(2,1)} %copy.123), calls=%async_computation.7 | async-start | bytes 8257536 | tf_op jit(solution)/shard_map/all_to_all | solution.py:121
  237.6 4.3 %all-to-all-start.2 = ((bf16[8,4,16,576]{3,2,1,0:T(8,128)(2,1)}), bf16[8,4,16,576]{3,2,1,0:T(8,128)(2,1)S(1)}, u32[]{:S(2)}, u32[]{:S(2)}) async-start(bf16[8,4,16,576]{3,2,1,0:T(8,128)(2,1)} %reshape_reshape.18), calls=%async_computation.2 | async-start | bytes 1310720 | tf_op jit(solution)/shard_map/all_to_all | solution.py:121
  241.9 3.8 fusion.26
  245.8 7.9 %all-to-all-done.2 = bf16[8,4,16,576]{3,2,1,0:T(8,128)(2,1)S(1)} async-done(((bf16[8,4,16,576]{3,2,1,0:T(8,128)(2,1)}), bf16[8,4,16,576]{3,2,1,0:T(8,128)(2,1)S(1)}, u32[]{:S(2)}, u32[]{:S(2)}) %all-to-all-start.2) | async-done | bytes 589856 | tf_op jit(solution)/shard_map/all_to_all | solution.py:121
  253.7 4.5 %all-to-all-start.6 = ((bf16[4,144,1152]{2,1,0:T(8,128)(2,1)}), bf16[4,144,1152]{2,1,0:T(8,128)(2,1)}, u32[]{:S(2)}, u32[]{:S(2)}) async-start(bf16[4,144,1152]{2,1,0:T(8,128)(2,1)} %fusion.26), calls=%async_computation.6 | async-start | bytes 2654208 | tf_op jit(solution)/shard_map/all_to_all | solution.py:121
  262.9 13.4 %all-to-all-done.6 = bf16[4,144,1152]{2,1,0:T(8,128)(2,1)} async-done(((bf16[4,144,1152]{2,1,0:T(8,128)(2,1)}), bf16[4,144,1152]{2,1,0:T(8,128)(2,1)}, u32[]{:S(2)}, u32[]{:S(2)}) %all-to-all-start.6) | async-done | bytes 1327136 | tf_op jit(solution)/shard_map/all_to_all | solution.py:121
  276.4 4.2 %all-to-all-start.4 = ((bf16[8,4,16,1152]{3,2,1,0:T(8,128)(2,1)}), bf16[8,4,16,1152]{3,2,1,0:T(8,128)(2,1)}, u32[]{:S(2)}, u32[]{:S(2)}) async-start(bf16[8,4,16,1152]{3,2,1,0:T(8,128)(2,1)} %bitcast.251), calls=%async_computation.4 | async-start | bytes 2359296 | tf_op jit(solution)/shard_map/all_to_all | solution.py:121
  287.5 4.2 %reshape.295 = bf16[32,36,144]{1,0,2:T(8,128)(2,1)} reshape(bf16[1152,144]{0,1:T(8,128)(2,1)S(1)} %fusion.57) | data formatting | bytes 663552 | tf_op jit(solution)/shard_map/reshape | solution.py:244
  291.7 6.3 %all-to-all-done.4 = bf16[8,4,16,1152]{3,2,1,0:T(8,128)(2,1)} async-done(((bf16[8,4,16,1152]{3,2,1,0:T(8,128)(2,1)}), bf16[8,4,16,1152]{3,2,1,0:T(8,128)(2,1)}, u32[]{:S(2)}, u32[]{:S(2)}) %all-to-all-start.4) | async-done | bytes 1179680 | tf_op jit(solution)/shard_map/all_to_all | solution.py:121
  298.0 4.4 %all-to-all-start.8 = ((bf16[4,144,1728]{2,1,0:T(8,128)(2,1)}), bf16[4,144,1728]{2,1,0:T(8,128)(2,1)}, u32[]{:S(2)}, u32[]{:S(2)}) async-start(bf16[4,144,1728]{2,1,0:T(8,128)(2,1)} %fusion.17), calls=%async_computation.8 | async-start | bytes 4128768 | tf_op jit(solution)/shard_map/all_to_all | solution.py:121
  311.4 17.2 %all-to-all-done.8 = bf16[4,144,1728]{2,1,0:T(8,128)(2,1)} async-done(((bf16[4,144,1728]{2,1,0:T(8,128)(2,1)}), bf16[4,144,1728]{2,1,0:T(8,128)(2,1)}, u32[]{:S(2)}, u32[]{:S(2)}) %all-to-all-start.8) | async-done | bytes 1990688 | tf_op jit(solution)/shard_map/all_to_all | solution.py:121
  331.5 5.4 %reshape.269 = bf16[32,54,144]{1,0,2:T(8,128)(2,1)} reshape(bf16[1728,144]{0,1:T(8,128)(2,1)} %fusion.56) | data formatting | bytes 995328 | tf_op jit(solution)/shard_map/reshape | solution.py:245
  340.7 6.5 %all-to-all-start.9 = ((bf16[32,90,144]{1,2,0:T(8,128)(2,1)}), bf16[32,90,144]{1,2,0:T(8,128)(2,1)}, u32[]{:S(2)}, u32[]{:S(2)}) async-start(bf16[32,90,144]{1,2,0:T(8,128)(2,1)} %copy.125), calls=%async_computation.9 | async-start | bytes 2359296 | tf_op jit(solution)/shard_map/all_to_all | solution.py:121
  355.4 22.0 %all-to-all-done.9 = bf16[32,90,144]{1,2,0:T(8,128)(2,1)} async-done(((bf16[32,90,144]{1,2,0:T(8,128)(2,1)}), bf16[32,90,144]{1,2,0:T(8,128)(2,1)}, u32[]{:S(2)}, u32[]{:S(2)}) %all-to-all-start.9) | async-done | bytes 829472 | tf_op jit(solution)/shard_map/all_to_all | solution.py:121
  (162 shorter events, 110.8 us)
Async XLA Ops:
  7.2 19.0 %copy-start.20 = (bf16[1,4,128,1728]{2,3,1,0:T(8,128)(2,1)S(1)}, bf16[1,4,128,1728]{2,3,1,0:T(8,128)(2,1)}, u32[]{:S(2)}) copy-start(bf16[1,4,128,1728]{2,3,1,0:T(8,128)(2,1)} %param.11) | copy-start | bytes 5308420
  7.2 111.2 %all-gather.6.cloned.1.call-start = ((), (), s32[]{:S(2)}) async-start(), calls=%async_computation.10 | async-start | bytes 7299072 | tf_op jit(solution)/shard_map/all_gather | solution.py:113
  28.4 2.1 copy-start.28
  32.0 6.2 %copy-start.4 = (bf16[1,4,128,1152]{3,2,1,0:T(8,128)(2,1)S(1)}, bf16[1,4,128,1152]{3,2,1,0:T(8,128)(2,1)}, u32[]{:S(2)}) copy-start(bf16[1,4,128,1152]{3,2,1,0:T(8,128)(2,1)} %param.16) | copy-start | bytes 3538948
  33.8 15.5 %all-to-all-start.1 = ((bf16[8,4,16,576]{3,2,1,0:T(8,128)(2,1)}), bf16[8,4,16,576]{3,2,1,0:T(8,128)(2,1)S(1)}, u32[]{:S(2)}, u32[]{:S(2)}) async-start(bf16[8,4,16,576]{3,2,1,0:T(8,128)(2,1)} %copy.92), calls=%async_computation.1 | async-start | bytes 1310720 | tf_op jit(solution)/shard_map/all_to_all | solution.py:121
  38.2 14.8 %copy-start.16 = (bf16[1,4,128,1152]{3,2,1,0:T(8,128)(2,1)S(1)}, bf16[1,4,128,1152]{3,2,1,0:T(8,128)(2,1)}, u32[]{:S(2)}) copy-start(bf16[1,4,128,1152]{3,2,1,0:T(8,128)(2,1)} %param.10) | copy-start | bytes 3538948
  49.3 4.9 %copy-start.22 = (bf16[8,4,16,576]{3,2,1,0:T(8,128)(2,1)}, bf16[8,4,16,576]{3,2,1,0:T(8,128)(2,1)S(1)}, u32[]{:S(2)}) copy-start(bf16[8,4,16,576]{3,2,1,0:T(8,128)(2,1)S(1)} %all-to-all-done.1) | copy-start | bytes 1769476
  49.3 5.1 %copy-start.25 = (f32[1,3,1152]{2,0,1:T(1,128)S(1)}, f32[1,3,1152]{2,0,1:T(1,128)}, u32[]{:S(2)}) copy-start(f32[1,3,1152]{2,0,1:T(1,128)} %param.15) | copy-start | bytes 41476
  49.3 21.0 %all-to-all-start.3 = ((bf16[8,4,16,1152]{3,2,1,0:T(8,128)(2,1)}), bf16[8,4,16,1152]{3,2,1,0:T(8,128)(2,1)S(1)}, u32[]{:S(2)}, u32[]{:S(2)}) async-start(bf16[8,4,16,1152]{3,2,1,0:T(8,128)(2,1)} %bitcast.244), calls=%async_computation.3 | async-start | bytes 2359296 | tf_op jit(solution)/shard_map/all_to_all | solution.py:121
  70.3 6.1 %copy-start.2 = (bf16[8,4,16,1152]{3,2,1,0:T(8,128)(2,1)}, bf16[8,4,16,1152]{3,2,1,0:T(8,128)(2,1)S(1)}, u32[]{:S(2)}) copy-start(bf16[8,4,16,1152]{3,2,1,0:T(8,128)(2,1)S(1)} %all-to-all-done.3) | copy-start | bytes 3538948
  70.3 52.2 %all-to-all-start = ((bf16[8,4,16,1152]{3,2,1,0:T(8,128)(2,1)}), bf16[8,4,16,1152]{3,2,1,0:T(8,128)(2,1)}, u32[]{:S(2)}, u32[]{:S(2)}) async-start(bf16[8,4,16,1152]{3,2,1,0:T(8,128)(2,1)} %bitcast.245), calls=%async_computation | async-start | bytes 2359296 | tf_op jit(solution)/shard_map/all_to_all | solution.py:121
  118.4 1.8 slice-start
  125.6 12.5 %copy-start = (f32[32,16,1152]{2,1,0:T(8,128)}, f32[32,16,1152]{2,1,0:T(8,128)S(1)}, u32[]{:S(2)}) copy-start(f32[32,16,1152]{2,1,0:T(8,128)S(1)} %get-tuple-element.29) | copy-start | bytes 7077892
  151.9 2.9 copy-start.6
  151.9 3.2 copy-start.18
  157.7 4.1 %copy-start.9 = (bf16[32,16,1,8,72]{4,3,2,1,0:T(8,128)(2,1)S(1)}, bf16[32,16,1,8,72]{4,3,2,1,0:T(8,128)(2,1)}, u32[]{:S(2)}) copy-start(bf16[32,16,1,8,72]{4,3,2,1,0:T(8,128)(2,1)} %get-tuple-element.19) | copy-start | bytes 1769476
  157.7 4.1 %copy-start.10 = (bf16[32,16,1,8,72]{4,3,2,1,0:T(8,128)(2,1)S(1)}, bf16[32,16,1,8,72]{4,3,2,1,0:T(8,128)(2,1)}, u32[]{:S(2)}) copy-start(bf16[32,16,1,8,72]{4,3,2,1,0:T(8,128)(2,1)} %get-tuple-element.20) | copy-start | bytes 1769476
  165.1 5.4 %copy-start.19 = (bf16[32,16,1,8,72]{4,3,2,1,0:T(8,128)(2,1)S(1)}, bf16[32,16,1,8,72]{4,3,2,1,0:T(8,128)(2,1)}, u32[]{:S(2)}) copy-start(bf16[32,16,1,8,72]{4,3,2,1,0:T(8,128)(2,1)} %get-tuple-element.21) | copy-start | bytes 1769476
  165.1 5.4 %copy-start.27 = (f32[16,8,32,32]{2,3,1,0:T(8,128)S(1)}, f32[16,8,32,32]{2,3,1,0:T(8,128)}, u32[]{:S(2)}) copy-start(f32[16,8,32,32]{2,3,1,0:T(8,128)} %get-tuple-element.31) | copy-start | bytes 1572868
  175.9 5.1 %copy-start.11 = (bf16[32,16,1,8,72]{4,0,3,1,2:T(8,128)(2,1)S(1)}, bf16[32,16,1,8,72]{4,0,3,1,2:T(8,128)(2,1)}, u32[]{:S(2)}) copy-start(bf16[32,16,1,8,72]{4,0,3,1,2:T(8,128)(2,1)} %fusion.24) | copy-start | bytes 1769476
  191.4 3.4 copy-start.1
  194.8 5.5 %copy-start.3 = (bf16[8,4,16,1152]{3,2,1,0:T(8,128)(2,1)S(1)}, bf16[8,4,16,1152]{3,2,1,0:T(8,128)(2,1)}, u32[]{:S(2)}) copy-start(bf16[8,4,16,1152]{3,2,1,0:T(8,128)(2,1)} %copy-done.2) | copy-start | bytes 3538948
  200.3 2.0 copy-start.23
  206.4 21.1 %all-to-all-start.5 = ((bf16[2,4,144,1152]{3,2,1,0:T(8,128)(2,1)}), bf16[2,4,144,1152]{3,2,1,0:T(8,128)(2,1)S(1)}, u32[]{:S(2)}, u32[]{:S(2)}) async-start(bf16[2,4,144,1152]{3,2,1,0:T(8,128)(2,1)} %copy_bitcast_fusion), calls=%async_computation.5 | async-start | bytes 5308416 | tf_op jit(solution)/shard_map/all_to_all | solution.py:121
  227.5 10.1 %all-to-all-start.7 = ((bf16[2,4,144,1728]{3,2,1,0:T(8,128)(2,1)}), bf16[2,4,144,1728]{3,2,1,0:T(8,128)(2,1)}, u32[]{:S(2)}, u32[]{:S(2)}) async-start(bf16[2,4,144,1728]{3,2,1,0:T(8,128)(2,1)} %copy.123), calls=%async_computation.7 | async-start | bytes 8257536 | tf_op jit(solution)/shard_map/all_to_all | solution.py:121
  237.6 16.0 %all-to-all-start.2 = ((bf16[8,4,16,576]{3,2,1,0:T(8,128)(2,1)}), bf16[8,4,16,576]{3,2,1,0:T(8,128)(2,1)S(1)}, u32[]{:S(2)}, u32[]{:S(2)}) async-start(bf16[8,4,16,576]{3,2,1,0:T(8,128)(2,1)} %reshape_reshape.18), calls=%async_computation.2 | async-start | bytes 1310720 | tf_op jit(solution)/shard_map/all_to_all | solution.py:121
  253.7 22.7 %all-to-all-start.6 = ((bf16[4,144,1152]{2,1,0:T(8,128)(2,1)}), bf16[4,144,1152]{2,1,0:T(8,128)(2,1)}, u32[]{:S(2)}, u32[]{:S(2)}) async-start(bf16[4,144,1152]{2,1,0:T(8,128)(2,1)} %fusion.26), calls=%async_computation.6 | async-start | bytes 2654208 | tf_op jit(solution)/shard_map/all_to_all | solution.py:121
  261.2 19.4 %copy-start.7 = (bf16[1152,1152]{1,0:T(8,128)(2,1)S(1)}, bf16[1152,1152]{1,0:T(8,128)(2,1)}, u32[]{:S(2)}) copy-start(bf16[1152,1152]{1,0:T(8,128)(2,1)} %reshape.259) | copy-start | bytes 7962628
  276.4 21.6 %all-to-all-start.4 = ((bf16[8,4,16,1152]{3,2,1,0:T(8,128)(2,1)}), bf16[8,4,16,1152]{3,2,1,0:T(8,128)(2,1)}, u32[]{:S(2)}, u32[]{:S(2)}) async-start(bf16[8,4,16,1152]{3,2,1,0:T(8,128)(2,1)} %bitcast.251), calls=%async_computation.4 | async-start | bytes 2359296 | tf_op jit(solution)/shard_map/all_to_all | solution.py:121
  298.0 30.6 %all-to-all-start.8 = ((bf16[4,144,1728]{2,1,0:T(8,128)(2,1)}), bf16[4,144,1728]{2,1,0:T(8,128)(2,1)}, u32[]{:S(2)}, u32[]{:S(2)}) async-start(bf16[4,144,1728]{2,1,0:T(8,128)(2,1)} %fusion.17), calls=%async_computation.8 | async-start | bytes 4128768 | tf_op jit(solution)/shard_map/all_to_all | solution.py:121
  340.7 36.7 %all-to-all-start.9 = ((bf16[32,90,144]{1,2,0:T(8,128)(2,1)}), bf16[32,90,144]{1,2,0:T(8,128)(2,1)}, u32[]{:S(2)}, u32[]{:S(2)}) async-start(bf16[32,90,144]{1,2,0:T(8,128)(2,1)} %copy.125), calls=%async_computation.9 | async-start | bytes 2359296 | tf_op jit(solution)/shard_map/all_to_all | solution.py:121
  347.2 2.7 copy-start.21
  (10 other events, 14.1 us)
Sparse Core Ops, SparseCore 0:
  25.0 93.3 all-gather.5

commit v2 on v1

v2 whole, which is shorter than its diff:
```python
import functools
import math

import jax
import jax.numpy as jnp
from jax import lax
from jax.experimental import pallas as pl
from jax.experimental.pallas import tpu as pltpu
from jax.sharding import Mesh
from jax.sharding import PartitionSpec as P

HEAD_DIM = 72
EPSILON = 1e-06
NEGATIVE = -1e30
LANES = 128
VMEM_BYTES = 56 * 1024 * 1024
F32 = jnp.float32
BF16 = jnp.bfloat16


def dot_nn(left, right):
    return lax.dot_general(left, right, (((1,), (0,)), ((), ())), preferred_element_type=F32)


def dot_nt(left, right):
    return lax.dot_general(left, right, (((1,), (1,)), ((), ())), preferred_element_type=F32)


def dot_tn(left, right):
    return lax.dot_general(left, right, (((0,), (0,)), ((), ())), preferred_element_type=F32)


def head_windows(inner):
    windows = []
    for head in range(inner // HEAD_DIM):
        low = head * HEAD_DIM
        start = low // LANES * LANES
        stop = min(-(-(low + HEAD_DIM) // LANES) * LANES, inner)
        windows.append((start, stop, low - start))
    return windows


def own_lanes(window):
    start, stop, offset = window
    lane = lax.broadcasted_iota(jnp.int32, (1, stop - start), 1)
    return (lane >= offset) & (lane < offset + HEAD_DIM)


def only(lanes, rows):
    return jnp.where(lanes, rows, jnp.zeros((), rows.dtype))


def softmax_rows(query, key, allowed):
    logits = dot_nt(query, key) * (1.0 / math.sqrt(HEAD_DIM))
    logits = jnp.where(allowed, logits, NEGATIVE)
    powers = jnp.exp(logits - jnp.max(logits, axis=1, keepdims=True))
    return powers * (1.0 / jnp.sum(powers, axis=1, keepdims=True))


def attend_heads(query, key, value, allowed, out_acc):
    out_acc[...] = jnp.zeros(out_acc.shape, F32)
    for window in head_windows(query.shape[1]):
        start, stop, _ = window
        lanes = own_lanes(window)
        probs = softmax_rows(query[:, start:stop], only(lanes, key[:, start:stop]), allowed)
        out_acc[:, start:stop] += dot_nn(probs.astype(BF16), only(lanes, value[:, start:stop]))


def attend_heads_back(query, key, value, out, out_grad, allowed, q_acc, k_acc, v_acc):
    factor = 1.0 / math.sqrt(HEAD_DIM)
    for acc in (q_acc, k_acc, v_acc):
        acc[...] = jnp.zeros(acc.shape, F32)
    for window in head_windows(query.shape[1]):
        start, stop, _ = window
        lanes = own_lanes(window)
        key_h = only(lanes, key[:, start:stop])
        grad_h = only(lanes, out_grad[:, start:stop])
        probs = softmax_rows(query[:, start:stop], key_h, allowed)
        prob_grad = dot_nt(grad_h, value[:, start:stop])
        row_delta = jnp.sum(
            grad_h.astype(F32) * out[:, start:stop].astype(F32), axis=1, keepdims=True
        )
        logit_grad = (probs * (prob_grad - row_delta)).astype(BF16)
        q_acc[:, start:stop] += dot_nn(logit_grad, key_h) * factor
        k_acc[:, start:stop] += dot_tn(logit_grad, only(lanes, query[:, start:stop])) * factor
        v_acc[:, start:stop] += dot_tn(probs.astype(BF16), grad_h)


def slot_masks(info_ref, rows, slots):
    frames, limit, first = info_ref[0], info_ref[1], info_ref[2]
    group = pl.program_id(0)
    row = lax.broadcasted_iota(jnp.int32, (rows, 1), 0)
    slot = first + group * slots + row % slots
    token = (row // slots < frames) & (slot < limit)
    col = lax.broadcasted_iota(jnp.int32, (1, rows), 1)
    allowed = (row % slots == col % slots) & (col // slots < frames)
    return token.astype(F32), allowed


def normalised(mixed):
    values = mixed.astype(F32)
    centred = values - jnp.mean(values, axis=1, keepdims=True)
    inv_std = lax.rsqrt(jnp.mean(centred * centred, axis=1, keepdims=True) + EPSILON)
    return centred * inv_std, inv_std


def temporal_forward(
    info, mod, stream, out_s, w_spatial, w_qkv, mixed_ref, mod_ref, qkv_ref, out_ref, acc, slots
):
    rows, inner = acc.shape
    width = w_spatial.shape[0]
    token, allowed = slot_masks(info, rows, slots)
    branch = dot_nt(out_s[...].reshape(rows, inner), w_spatial[...])
    mixed = (stream[...].reshape(rows, width).astype(F32) + token * branch).astype(BF16)
    mixed_ref[...] = mixed.reshape(mixed_ref.shape)
    normed, _ = normalised(mixed)
    modulated = (normed * (1.0 + mod[0, 1:2]) + mod[0, 0:1]).astype(BF16)
    mod_ref[...] = modulated.reshape(mod_ref.shape)
    qkv = dot_nt(modulated, w_qkv[...]).astype(BF16)
    qkv_ref[...] = qkv.reshape(qkv_ref.shape)
    attend_heads(
        qkv[:, :inner], qkv[:, inner : 2 * inner], qkv[:, 2 * inner :], allowed, acc
    )
    out_ref[...] = acc[...].astype(BF16).reshape(out_ref.shape)


def temporal_backward(
    info, mod, grad, qkv_ref, out_t, modulated, w_temporal, dqkv_ref, g_temporal, g_qkv,
    q_acc, k_acc, v_acc, sum_t, sum_q, slots
):
    rows, inner = q_acc.shape
    width = w_temporal.shape[0]
    token, allowed = slot_masks(info, rows, slots)
    branch_grad = (token * mod[0, 2:3] * grad[...].reshape(rows, width).astype(F32)).astype(BF16)
    out_grad = dot_nn(branch_grad, w_temporal[...]).astype(BF16)
    qkv = qkv_ref[...].reshape(rows, 3 * inner)
    out = out_t[...].reshape(rows, inner)
    attend_heads_back(
        qkv[:, :inner], qkv[:, inner : 2 * inner], qkv[:, 2 * inner :], out, out_grad, allowed,
        q_acc, k_acc, v_acc,
    )
    dqkv = jnp.concatenate([q_acc[...], k_acc[...], v_acc[...]], axis=1).astype(BF16)
    dqkv_ref[...] = dqkv.reshape(dqkv_ref.shape)
    part_t = dot_tn(out, branch_grad)
    part_q = dot_tn(modulated[...].reshape(rows, width), dqkv)

    @pl.when(pl.program_id(0) == 0)
    def _():
        sum_t[...] = part_t
        sum_q[...] = part_q

    @pl.when(pl.program_id(0) > 0)
    def _():
        sum_t[...] += part_t
        sum_q[...] += part_q

    @pl.when(pl.program_id(0) == pl.num_programs(0) - 1)
    def _():
        g_temporal[...] = sum_t[...].astype(BF16)
        g_qkv[...] = sum_q[...].astype(BF16)


def norm_backward(
    info, mod, grad, mixed, out_s, dqkv, w_qkv, ln_ref, g_spatial, sum_s, slots
):
    rows = dqkv.shape[1]
    width = w_qkv.shape[1]
    token, _ = slot_masks(info, rows, slots)
    norm_grad = dot_nn(dqkv[...].reshape(rows, -1), w_qkv[...]) * (1.0 + mod[0, 1:2])
    normed, inv_std = normalised(mixed[...].reshape(rows, width))
    first = jnp.mean(norm_grad, axis=1, keepdims=True)
    second = jnp.mean(norm_grad * normed, axis=1, keepdims=True)
    ln_grad = (inv_std * (norm_grad - first - normed * second)).astype(BF16)
    ln_ref[...] = ln_grad.reshape(ln_ref.shape)
    grad_f = grad[...].reshape(rows, width).astype(F32)
    hidden_grad = (grad_f + ln_grad.astype(F32)).astype(BF16)
    branch_grad = (token * hidden_grad.astype(F32)).astype(BF16)
    part = dot_tn(out_s[...].reshape(rows, -1), branch_grad)

    @pl.when(pl.program_id(0) == 0)
    def _():
        sum_s[...] = part

    @pl.when(pl.program_id(0) > 0)
    def _():
        sum_s[...] += part

    @pl.when(pl.program_id(0) == pl.num_programs(0) - 1)
    def _():
        g_spatial[...] = sum_s[...].astype(BF16)


def frame_keys(info_ref, rows):
    return lax.broadcasted_iota(jnp.int32, (1, rows), 1) < info_ref[1]


def frame_tokens(info_ref, rows):
    row = lax.broadcasted_iota(jnp.int32, (rows, 1), 0)
    alive = info_ref[3] + pl.program_id(0) < info_ref[0]
    return ((row < info_ref[1]) & alive).astype(F32)


def spatial_forward(info, qkv_ref, out_ref, acc):
    rows, inner = acc.shape
    qkv = qkv_ref[0]
    attend_heads(
        qkv[:, :inner], qkv[:, inner : 2 * inner], qkv[:, 2 * inner :], frame_keys(info, rows), acc
    )
    out_ref[0] = acc[...].astype(BF16)


def block_forward(info, mod, stream, out_s, out_t, w_spatial, w_temporal, block_ref):
    rows = stream.shape[1]
    token = frame_tokens(info, rows)
    mixed = (stream[0].astype(F32) + token * dot_nt(out_s[0], w_spatial[...])).astype(BF16)
    branch = dot_nt(out_t[0], w_temporal[...])
    block_ref[0] = (mixed.astype(F32) + token * mod[0, 2:3] * branch).astype(BF16)


def spatial_backward(
    info, grad, ln_grad, qkv_ref, out_s, w_spatial, hidden_ref, dqkv_ref, q_acc, k_acc, v_acc
):
    rows, inner = q_acc.shape
    hidden_grad = (grad[0].astype(F32) + ln_grad[0].astype(F32)).astype(BF16)
    hidden_ref[0] = hidden_grad
    branch_grad = (frame_tokens(info, rows) * hidden_grad.astype(F32)).astype(BF16)
    out_grad = dot_nn(branch_grad, w_spatial[...]).astype(BF16)
    qkv = qkv_ref[0]
    attend_heads_back(
        qkv[:, :inner], qkv[:, inner : 2 * inner], qkv[:, 2 * inner :], out_s[0], out_grad,
        frame_keys(info, rows), q_acc, k_acc, v_acc,
    )
    dqkv_ref[0] = jnp.concatenate([q_acc[...], k_acc[...], v_acc[...]], axis=1).astype(BF16)


def whole(array):
    return pl.BlockSpec(array.shape, lambda step: (0,) * array.ndim)


def per_frame(array):
    return pl.BlockSpec((1,) + array.shape[1:], lambda step: (step, 0, 0))


def per_group(array):
    return pl.BlockSpec(
        (array.shape[0], 1) + array.shape[2:], lambda step: (0, step, 0, 0)
    )


SCALARS = pl.BlockSpec(memory_space=pltpu.SMEM)


def run(body, steps, operands, specs, results, result_specs, scratch, flops):
    leaves = operands + jax.tree.leaves(results)
    moved = sum(math.prod(a.shape) * a.dtype.itemsize for a in leaves)
    return pl.pallas_call(
        body,
        grid=(steps,),
        in_specs=specs,
        out_specs=result_specs,
        out_shape=results,
        scratch_shapes=scratch,
        compiler_params=pltpu.CompilerParams(vmem_limit_bytes=VMEM_BYTES),
        cost_estimate=pl.CostEstimate(flops=flops, bytes_accessed=moved, transcendentals=0),
    )(*operands)


def shape_of(*dims, dtype=BF16):
    return jax.ShapeDtypeStruct(dims, dtype)


def weight_rows(out_spatial, qkv_temporal, out_temporal):
    packed = jnp.concatenate(
        [jnp.concatenate([out_spatial.T, out_temporal.T], axis=1), qkv_temporal.T], axis=0
    )
    near = lax.all_gather(packed, ("y", "c"), axis=0, tiled=False)
    narrow = out_spatial.shape[1]
    half = out_spatial.shape[0]
    pair = jnp.transpose(near[:, :narrow], (1, 0, 2))
    first = pair[:, :, :half].reshape(narrow, -1)
    second = pair[:, :, half:].reshape(narrow, -1)
    wide = jnp.transpose(near[:, narrow:], (1, 0, 2)).reshape(near.shape[1] - narrow, -1)
    rows = jnp.concatenate([jnp.concatenate([first, second], axis=1), wide], axis=0)
    far = lax.all_gather(rows, ("x", "z"), axis=0, tiled=False)
    inner = first.shape[1]
    w_pair = far[:, :narrow].reshape(-1, 2 * inner)
    w_wide = far[:, narrow:].reshape(-1, far.shape[2])
    return (w_pair[:, :inner], w_wide, w_pair[:, inner:])


def exchange(rows, axes):
    return lax.all_to_all(rows, axes, 0, 0, tiled=True)


def halve_and_quarter(terms):
    split = terms.reshape((4, 2) + terms.shape[1:])
    split = jnp.transpose(split, (1, 0, 2, 3))
    pairs = exchange(split, "c").astype(F32)
    pairs = (pairs[0] + pairs[1]).astype(BF16)
    quads = exchange(pairs, "y").astype(F32)
    return ((quads[0] + quads[1]) + (quads[2] + quads[3])).astype(BF16)


def reduce_grads(g_spatial, g_qkv, g_temporal):
    seq_count = lax.axis_size(("y", "c"))
    dp_count = lax.axis_size(("x", "z"))
    width = g_spatial.shape[1]
    sum_qkv = halve_and_quarter(g_qkv.reshape(seq_count, -1, g_qkv.shape[1]))
    pair = [g.reshape(seq_count, -1, width) for g in (g_spatial, g_temporal)]
    sum_pair = halve_and_quarter(jnp.concatenate(pair, axis=1))
    chunks = jnp.concatenate(
        [
            sum_pair.T.reshape(dp_count, -1, sum_pair.shape[0]),
            sum_qkv.T.reshape(dp_count, -1, sum_qkv.shape[0]),
        ],
        axis=1,
    )
    total = jnp.sum(exchange(chunks, ("x", "z")).astype(F32), axis=0)
    narrow = width // dp_count
    half = sum_pair.shape[0] // 2
    return (total[:narrow, :half].T, total[narrow:].T, total[:narrow, half:].T)


def on_device(
    hidden,
    spatial_qkv,
    out_spatial,
    qkv_temporal,
    out_temporal,
    modulation,
    cotangent,
    frame_count,
    patch_height,
    patch_width,
):
    seq_count = lax.axis_size(("y", "c"))
    seq_place = lax.axis_index(("y", "c"))
    stream = hidden[0]
    grad_out = cotangent[0]
    packed_qkv = spatial_qkv[0]
    frame_dev, slot_total, width = stream.shape
    slot_dev = slot_total // seq_count
    inner = out_spatial.shape[0] * seq_count
    slots = 8
    groups = slot_dev // slots
    rows = frame_dev * seq_count * slots
    info = jnp.stack(
        [
            frame_count[0],
            patch_height[0] * patch_width[0],
            seq_place * slot_dev,
            seq_place * frame_dev,
        ]
    ).astype(jnp.int32)

    def to_slots(tokens):
        split = tokens.reshape(frame_dev, seq_count, groups, slots, -1)
        split = jnp.transpose(split, (1, 2, 0, 3, 4))
        return exchange(split.reshape(seq_count, groups, frame_dev * slots, -1), ("y", "c"))

    def to_frames(tokens):
        moved = exchange(tokens, ("y", "c")).reshape(seq_count, groups, frame_dev, slots, -1)
        return jnp.transpose(moved, (2, 0, 1, 3, 4)).reshape(frame_dev, slot_total, -1)

    stream_s = to_slots(stream)
    frame_acc = pltpu.VMEM((slot_total, inner), F32)
    out_s = shape_of(frame_dev, slot_total, inner)
    out_s = run(
        spatial_forward,
        frame_dev,
        [info, packed_qkv],
        [SCALARS, per_frame(packed_qkv)],
        out_s,
        per_frame(out_s),
        [frame_acc],
        4 * frame_dev * slot_total * slot_total * inner,
    )
    out_s_s = to_slots(out_s)
    grad_s = to_slots(grad_out)
    w_spatial, w_qkv, w_temporal = weight_rows(out_spatial, qkv_temporal, out_temporal)

    group_acc = pltpu.VMEM((rows, inner), F32)
    result = (
        shape_of(groups, rows, width),
        shape_of(groups, rows, width),
        shape_of(groups, rows, 3 * inner),
        shape_of(seq_count, groups, rows // seq_count, inner),
    )
    tokens = groups * rows
    mixed_s, modulated, qkv_t, out_t = run(
        functools.partial(temporal_forward, slots=slots),
        groups,
        [info, modulation, stream_s, out_s_s, w_spatial, w_qkv],
        [SCALARS, whole(modulation), per_group(stream_s), per_group(out_s_s), whole(w_spatial), whole(w_qkv)],
        result,
        [per_frame(result[0]), per_frame(result[1]), per_frame(result[2]), per_group(result[3])],
        [group_acc],
        8 * tokens * width * inner + 4 * tokens * rows * inner,
    )
    out_t_f = to_frames(out_t)

    result = (
        shape_of(groups, rows, 3 * inner),
        shape_of(inner, width),
        shape_of(width, 3 * inner),
    )
    dqkv_t, g_temporal, g_qkv = run(
        functools.partial(temporal_backward, slots=slots),
        groups,
        [info, modulation, grad_s, qkv_t, out_t, modulated, w_temporal],
        [SCALARS, whole(modulation), per_group(grad_s), per_frame(qkv_t), per_group(out_t), per_frame(modulated), whole(w_temporal)],
        result,
        [per_frame(result[0]), whole(result[1]), whole(result[2])],
        [group_acc, group_acc, group_acc, pltpu.VMEM((inner, width), F32), pltpu.VMEM((width, 3 * inner), F32)],
        10 * tokens * width * inner + 10 * tokens * rows * inner,
    )
    result = (
        shape_of(seq_count, groups, rows // seq_count, width),
        shape_of(inner, width),
    )
    ln_grad, g_spatial = run(
        functools.partial(norm_backward, slots=slots),
        groups,
        [info, modulation, grad_s, mixed_s, out_s_s, dqkv_t, w_qkv],
        [SCALARS, whole(modulation), per_group(grad_s), per_frame(mixed_s), per_group(out_s_s), per_frame(dqkv_t), whole(w_qkv)],
        result,
        [per_group(result[0]), whole(result[1])],
        [pltpu.VMEM((inner, width), F32)],
        8 * tokens * width * inner,
    )
    ln_frames = to_frames(ln_grad)
    summed = reduce_grads(g_spatial, g_qkv, g_temporal)

    block_out = shape_of(frame_dev, slot_total, width)
    block_out = run(
        block_forward,
        frame_dev,
        [info, modulation, stream, out_s, out_t_f, w_spatial, w_temporal],
        [SCALARS, whole(modulation), per_frame(stream), per_frame(out_s), per_frame(out_t_f), whole(w_spatial), whole(w_temporal)],
        block_out,
        per_frame(block_out),
        [],
        4 * tokens * width * inner,
    )
    result = (shape_of(frame_dev, slot_total, width), shape_of(frame_dev, slot_total, 3 * inner))
    hidden_grad, qkv_s_grad = run(
        spatial_backward,
        frame_dev,
        [info, grad_out, ln_frames, packed_qkv, out_s, w_spatial],
        [SCALARS, per_frame(grad_out), per_frame(ln_frames), per_frame(packed_qkv), per_frame(out_s), whole(w_spatial)],
        result,
        [per_frame(result[0]), per_frame(result[1])],
        [frame_acc, frame_acc, frame_acc],
        2 * tokens * width * inner + 10 * tokens * slot_total * inner,
    )
    return (block_out[None], hidden_grad[None], qkv_s_grad[None], summed[0], summed[1], summed[2])


def solution(mesh):
    torus = Mesh(mesh.devices.reshape(4, 8, 4, 2), ("x", "z", "y", "c"))
    dp, seq = ("x", "z"), ("y", "c")
    tokens = P(dp, seq, None, None)
    weight = P(seq, dp)
    placed = (
        tokens,
        tokens,
        weight,
        weight,
        weight,
        P(dp, None, None),
        tokens,
        P(dp),
        P(dp),
        P(dp),
    )
    return jax.shard_map(
        on_device,
        mesh=torus,
        in_specs=placed,
        out_specs=(tokens, tokens, tokens, weight, weight, weight),
        check_vma=False,
    )
```

time: 394 us -> 343 us (0.87)
  Pallas kernels: 0 us -> 76.2 us
  matrix products: 53.4 us -> 0 us
  local copies, waits for them, and re-layouts: 89.2 us -> 57.4 us
  waiting for transfers between devices: 135 us -> 112 us
  other arithmetic: 34.8 us -> 21.8 us
    pallas_call x0 -> x6, Pallas kernels: none -> 76.2 us  [run(): pl.pallas_call(body, grid=(steps,), in_specs=specs, out_specs=result_spec...]
    dot_general x20 -> x0, matrix products: 47.9 us -> none  [the longest x4 13 us: product_by_transpose(): jnp.einsum('rd,cd->rc', left, right, preferred_element_type=jnp.float32)]
    all_to_all x10, waiting for transfers between devices: 94.2 us -> 76.3 us  [exchange(): return lax.all_to_all(rows, axes, 0, 0, tiled=True)]
    convert_element_type x5 -> x0, local copies, waits for them, and re-layouts: 12.3 us -> none  [the longest x1 6.44 us: on_device(): grad_qkv = transposed_product(flat_mod, qkv_t_grad).astype(jnp.bfloat16)]
    reshape x6 -> x5, local copies, waits for them, and re-layouts: 23.1 us -> 14.2 us  [the longest x1 4.64 us: reduce_grads(): sum_qkv.T.reshape(dp_count, -1, sum_qkv.shape[0])]
    convert_element_type x18 -> x6, other arithmetic: 23 us -> 14.6 us  [the longest x2 5.58 us: halve_and_quarter(): pairs = exchange(split, 'c').astype(F32)]
    sub x2 -> x0, matrix products: 5.5 us -> none  [attend(): powers = jnp.exp(logits - largest)]
    all_gather x1, waiting for transfers between devices: 40.6 us -> 35.2 us  [weight_rows(): far = lax.all_gather(rows, ('x', 'z'), axis=0, tiled=False)]
  transfers between devices with their start and end apart: 11 -> 11, of which waited for: 9 -> 8; matrix products, arithmetic and copies ran while one was open for 18% -> 20% of each run, Pallas kernels for 0% -> 14%
where the time goes in v2:
time: 343 us; the launch traced here: 341 us
  waiting for transfers between devices  112 us (33%)
  Pallas kernels  76.2 us (22%)
  local copies, waits for them, and re-layouts  57.4 us (17%)
  starting transfers between devices  44.3 us (13%)
  other arithmetic  21.8 us (6%)
  between operations  16.2 us (5%)
  blocking collectives  13.5 us (4%)
    all_to_all x10, waiting for transfers between devices, exchange(): return lax.all_to_all(rows, axes, 0, 0, tiled=True)  76.3 us
    pallas_call x6, Pallas kernels, run(): pl.pallas_call(body, grid=(steps,), in_specs=specs, out_specs=result_spec...  76.2 us
    all_to_all x10, starting transfers between devices, exchange(): return lax.all_to_all(rows, axes, 0, 0, tiled=True)  44.2 us
    all_gather x1, waiting for transfers between devices, weight_rows(): far = lax.all_gather(rows, ('x', 'z'), axis=0, tiled=False)  35.2 us
    all_gather x1, blocking collectives, weight_rows(): near = lax.all_gather(packed, ('y', 'c'), axis=0, tiled=False)  13.5 us
    unnamed x25, local copies, waits for them, and re-layouts  12.8 us
  transfers between devices with their start and end apart: 11, of which 8 were waited for; matrix products, arithmetic and copies ran while one was open for 20% of the time, Pallas kernels for 14%

profile of v2, /device:TPU:32, one launch (start us, length us, event | category | flops | bytes accessed | tf_op | source)
XLA Modules:
  0.0 340.9 jit_solution(13274022194370210081)
XLA Ops:
  9.8 13.5 %all-gather.2 = bf16[8,90,144]{1,2,0:T(8,128)(2,1)S(1)} all-gather(bf16[1,90,144]{1,2,0:T(8,128)(2,1)S(1)} %maximum_bitcast_fusion), channel_id=2, replica_groups=mesh['x'=4,'z'=8,'y'=4,'c'=2] {'y','c'}, dimensions={0}, use_global_device_ids=true | all-gather | bytes 233280 | tf_op jit(solution)/shard_map/all_gather | solution.py:276
  30.0 9.8 %shard_map.145.out_s = bf16[4,128,576]{2,1,0:T(8,128)(2,1)} custom-call(s32[4]{0:T(128)} %pad_add_fusion.info, bf16[4,128,1728]{2,1,0:T(8,128)(2,1)} %bitcast.78), custom_call_target="tpu_custom_call" | custom-call | flops 150994944 | bytes 2359312 | tf_op jit(solution)/shard_map/pallas_call | solution.py:256
  42.0 3.8 %all-to-all-start.1 = ((bf16[8,2,32,576]{3,2,1,0:T(8,128)(2,1)}), bf16[8,2,32,576]{3,2,1,0:T(8,128)(2,1)S(1)}, u32[]{:S(2)}, u32[]{:S(2)}) async-start(bf16[8,2,32,576]{3,2,1,0:T(8,128)(2,1)} %bitcast.77), calls=%async_computation.1 | async-start | bytes 1310720 | tf_op jit(solution)/shard_map/all_to_all | solution.py:292
  46.9 10.6 %all-to-all-done.1.out_s = bf16[8,2,32,576]{3,2,1,0:T(8,128)(2,1)S(1)} async-done(((bf16[8,2,32,576]{3,2,1,0:T(8,128)(2,1)}), bf16[8,2,32,576]{3,2,1,0:T(8,128)(2,1)S(1)}, u32[]{:S(2)}, u32[]{:S(2)}) %all-to-all-start.1) | async-done | bytes 589856 | tf_op jit(solution)/shard_map/all_to_all | solution.py:292
  57.5 3.6 %all-to-all-start = ((bf16[8,2,32,1152]{3,2,1,0:T(8,128)(2,1)}), bf16[8,2,32,1152]{3,2,1,0:T(8,128)(2,1)S(1)}, u32[]{:S(2)}, u32[]{:S(2)}) async-start(bf16[8,2,32,1152]{3,2,1,0:T(8,128)(2,1)} %bitcast.76), calls=%async_computation | async-start | bytes 2359296 | tf_op jit(solution)/shard_map/all_to_all | solution.py:292
  62.2 16.1 %all-to-all-done.stream = bf16[8,2,32,1152]{3,2,1,0:T(8,128)(2,1)S(1)} async-done(((bf16[8,2,32,1152]{3,2,1,0:T(8,128)(2,1)}), bf16[8,2,32,1152]{3,2,1,0:T(8,128)(2,1)S(1)}, u32[]{:S(2)}, u32[]{:S(2)}) %all-to-all-start) | async-done | bytes 1179680 | tf_op jit(solution)/shard_map/all_to_all | solution.py:292
  78.4 4.2 %all-to-all-start.3 = ((bf16[8,2,32,1152]{3,2,1,0:T(8,128)(2,1)}), bf16[8,2,32,1152]{3,2,1,0:T(8,128)(2,1)}, u32[]{:S(2)}, u32[]{:S(2)}) async-start(bf16[8,2,32,1152]{3,2,1,0:T(8,128)(2,1)} %bitcast.75), calls=%async_computation.3 | async-start | bytes 2359296 | tf_op jit(solution)/shard_map/all_to_all | solution.py:292
  83.2 35.2 %all-gather.6.cloned.1.call-done = bf16[32,90,1152]{2,1,0:T(8,128)(2,1)} async-done(((bf16[1,90,1152]{2,1,0:T(8,128)(2,1)}), bf16[32,90,1152]{2,1,0:T(8,128)(2,1)}) %all-gather.6.cloned.1.call-update) | async-done | bytes 6635536 | tf_op jit(solution)/shard_map/all_gather | solution.py:284
  118.4 3.7 %slice.96 = bf16[32,36,1152]{2,1,0:T(8,128)(2,1)} slice(bf16[32,90,1152]{2,1,0:T(8,128)(2,1)} %all-gather.6.cloned.1.call-done), slice={[0:32], [0:36], [0:1152]} | slice | bytes 5308416 | tf_op jit(solution)/shard_map/slice | solution.py:286
  122.1 3.6 %reshape.84 = bf16[1152,1152]{1,0:T(8,128)(2,1)S(1)} reshape(bf16[32,36,1152]{2,1,0:T(8,128)(2,1)} %slice.96) | data formatting | bytes 5308416 | tf_op jit(solution)/shard_map/reshape | solution.py:286
  125.7 6.6 %slice.98 = bf16[32,54,1152]{2,1,0:T(8,128)(2,1)} slice(bf16[32,90,1152]{2,1,0:T(8,128)(2,1)} %all-gather.6.cloned.1.call-done), slice={[0:32], [36:90], [0:1152]} | slice | bytes 7962624 | tf_op jit(solution)/shard_map/slice | solution.py:287
  132.3 5.0 %reshape.85.w_qkv = bf16[1728,1152]{1,0:T(8,128)(2,1)} reshape(bf16[32,54,1152]{2,1,0:T(8,128)(2,1)} %slice.98) | data formatting | bytes 7962624 | tf_op jit(solution)/shard_map/reshape | solution.py:287
  139.7 11.7 %shard_map.146 = (bf16[2,256,1152]{2,1,0:T(8,128)(2,1)}, bf16[2,256,1152]{2,1,0:T(8,128)(2,1)}, bf16[2,256,1728]{2,1,0:T(8,128)(2,1)}, bf16[8,2,32,576]{3,2,1,0:T(8,128)(2,1)}) custom-call(s32[4]{0:T(128)} %pad_add_fusion.info, f32[1,3,1152]{2,1,0:T(4,128)} %copy.56.mod, bf16[8,2,32,1152]{3,2,1,0:T(8,128)(2,1)} %copy-done.5, ...), custom_call_target="tpu_custom_call" | custom-call | flops 3019898880 | bytes 11810320 | tf_op jit(solution)/shard_map/pallas_call | solution.py:256
  151.4 19.4 %shard_map.148 = (bf16[2,256,1728]{2,1,0:T(8,128)(2,1)}, bf16[576,1152]{1,0:T(8,128)(2,1)}, bf16[1152,1728]{1,0:T(8,128)(2,1)}) custom-call(s32[4]{0:T(128)} %pad_add_fusion.info, f32[1,3,1152]{2,1,0:T(4,128)} %copy.56.mod, bf16[8,2,32,1152]{3,2,1,0:T(8,128)(2,1)} %all-to-all-done.3.grad, bf16[2,256,1728]{2,1,0:T(8,128)(2,1)} %get-tuple-element.19.qkv_ref, ...), custom_call_target="tpu_custom_call" | custom-call | flops 4152360960 | bytes 13137424 | tf_op jit(solution)/shard_map/pallas_call | solution.py:256
  170.8 10.0 %shard_map.149 = (bf16[8,2,32,1152]{3,2,1,0:T(8,128)(2,1)}, bf16[576,1152]{1,0:T(8,128)(2,1)}) custom-call(s32[4]{0:T(128)} %pad_add_fusion.info, f32[1,3,1152]{2,1,0:T(4,128)} %copy.56.mod, bf16[8,2,32,1152]{3,2,1,0:T(8,128)(2,1)} %all-to-all-done.3.grad, bf16[2,256,1152]{2,1,0:T(8,128)(2,1)} %get-tuple-element.18.mixed, bf16[8,2,32,576]{3,2,1,0:T(8,128)(2,1)} %copy-done.6, ...), custom_call_target="tpu_custom_call" | custom-call | flops 2717908992 | bytes 11220496 | tf_op jit(solution)/shard_map/pallas_call | solution.py:256
  184.0 3.9 %all-to-all-start.5 = ((bf16[2,4,144,1152]{3,2,1,0:T(8,128)(2,1)}), bf16[2,4,144,1152]{3,2,1,0:T(8,128)(2,1)S(1)}, u32[]{:S(2)}, u32[]{:S(2)}) async-start(bf16[2,4,144,1152]{3,2,1,0:T(8,128)(2,1)} %copy_bitcast_fusion.1), calls=%async_computation.5 | async-start | bytes 5308416 | tf_op jit(solution)/shard_map/all_to_all | solution.py:292
  187.8 4.5 %copy.86 = bf16[4,2,144,1728]{3,2,0,1:T(8,128)(2,1)} copy(bf16[4,2,144,1728]{3,2,1,0:T(8,128)(2,1)} %bitcast.87) | data formatting | bytes 7962624 | tf_op jit(solution)/shard_map/reshape;reshape | solution.py:296
  192.3 5.8 %all-to-all-start.7 = ((bf16[2,4,144,1728]{3,2,1,0:T(8,128)(2,1)}), bf16[2,4,144,1728]{3,2,1,0:T(8,128)(2,1)}, u32[]{:S(2)}, u32[]{:S(2)}) async-start(bf16[2,4,144,1728]{3,2,1,0:T(8,128)(2,1)} %bitcast.80), calls=%async_computation.7 | async-start | bytes 8257536 | tf_op jit(solution)/shard_map/all_to_all | solution.py:292
  202.6 4.3 %all-to-all-start.2 = ((bf16[8,2,32,576]{3,2,1,0:T(8,128)(2,1)}), bf16[8,2,32,576]{3,2,1,0:T(8,128)(2,1)S(1)}, u32[]{:S(2)}, u32[]{:S(2)}) async-start(bf16[8,2,32,576]{3,2,1,0:T(8,128)(2,1)} %get-tuple-element.17.out_t), calls=%async_computation.2 | async-start | bytes 1310720 | tf_op jit(solution)/shard_map/all_to_all | solution.py:292
  206.9 3.8 %fusion.3 = bf16[4,144,1152]{2,1,0:T(8,128)(2,1)} fusion(f32[2,4,144,1152]{3,2,1,0:T(8,128)} %convert_element_type.39), kind=kLoop, calls=%fused_computation.9 | loop fusion | flops 1327104 | bytes 6635520 | tf_op jit(solution)/shard_map/convert_element_type | solution.py:299
  210.8 7.9 %all-to-all-done.2 = bf16[8,2,32,576]{3,2,1,0:T(8,128)(2,1)S(1)} async-done(((bf16[8,2,32,576]{3,2,1,0:T(8,128)(2,1)}), bf16[8,2,32,576]{3,2,1,0:T(8,128)(2,1)S(1)}, u32[]{:S(2)}, u32[]{:S(2)}) %all-to-all-start.2) | async-done | bytes 589856 | tf_op jit(solution)/shard_map/all_to_all | solution.py:292
  218.7 3.5 %all-to-all-start.6 = ((bf16[4,144,1152]{2,1,0:T(8,128)(2,1)}), bf16[4,144,1152]{2,1,0:T(8,128)(2,1)S(1)}, u32[]{:S(2)}, u32[]{:S(2)}) async-start(bf16[4,144,1152]{2,1,0:T(8,128)(2,1)} %fusion.3), calls=%async_computation.6 | async-start | bytes 2654208 | tf_op jit(solution)/shard_map/all_to_all | solution.py:292
  226.9 13.5 %all-to-all-done.6 = bf16[4,144,1152]{2,1,0:T(8,128)(2,1)S(1)} async-done(((bf16[4,144,1152]{2,1,0:T(8,128)(2,1)}), bf16[4,144,1152]{2,1,0:T(8,128)(2,1)S(1)}, u32[]{:S(2)}, u32[]{:S(2)}) %all-to-all-start.6) | async-done | bytes 1327136 | tf_op jit(solution)/shard_map/all_to_all | solution.py:292
  241.5 4.5 %all-to-all-start.8 = ((bf16[4,144,1728]{2,1,0:T(8,128)(2,1)}), bf16[4,144,1728]{2,1,0:T(8,128)(2,1)}, u32[]{:S(2)}, u32[]{:S(2)}) async-start(bf16[4,144,1728]{2,1,0:T(8,128)(2,1)} %fusion.2), calls=%async_computation.8 | async-start | bytes 4128768 | tf_op jit(solution)/shard_map/all_to_all | solution.py:292
  247.4 23.7 %all-to-all-done.8 = bf16[4,144,1728]{2,1,0:T(8,128)(2,1)} async-done(((bf16[4,144,1728]{2,1,0:T(8,128)(2,1)}), bf16[4,144,1728]{2,1,0:T(8,128)(2,1)}, u32[]{:S(2)}, u32[]{:S(2)}) %all-to-all-start.8) | async-done | bytes 1990688 | tf_op jit(solution)/shard_map/all_to_all | solution.py:292
  271.1 4.2 %all-to-all-start.4 = ((bf16[8,2,32,1152]{3,2,1,0:T(8,128)(2,1)}), bf16[8,2,32,1152]{3,2,1,0:T(8,128)(2,1)}, u32[]{:S(2)}, u32[]{:S(2)}) async-start(bf16[8,2,32,1152]{3,2,1,0:T(8,128)(2,1)} %get-tuple-element.22), calls=%async_computation.4 | async-start | bytes 2359296 | tf_op jit(solution)/shard_map/all_to_all | solution.py:292
  276.2 4.2 %reshape.101 = bf16[32,36,144]{1,0,2:T(8,128)(2,1)S(1)} reshape(bf16[1152,144]{0,1:T(8,128)(2,1)} %fusion.9) | data formatting | bytes 663552 | tf_op jit(solution)/shard_map/reshape | solution.py:313
  283.3 4.6 %reshape.92 = bf16[32,54,144]{1,0,2:T(8,128)(2,1)S(1)} reshape(bf16[1728,144]{0,1:T(8,128)(2,1)} %fusion.8) | data formatting | bytes 995328 | tf_op jit(solution)/shard_map/reshape | solution.py:314
  292.8 6.5 %all-to-all-start.9 = ((bf16[32,90,144]{1,2,0:T(8,128)(2,1)}), bf16[32,90,144]{1,2,0:T(8,128)(2,1)S(1)}, u32[]{:S(2)}, u32[]{:S(2)}) async-start(bf16[32,90,144]{1,2,0:T(8,128)(2,1)} %copy.66), calls=%async_computation.9 | async-start | bytes 2359296 | tf_op jit(solution)/shard_map/all_to_all | solution.py:292
  300.2 7.2 %shard_map.147 = bf16[4,128,1152]{2,1,0:T(8,128)(2,1)} custom-call(s32[4]{0:T(128)} %pad_add_fusion.info, f32[1,3,1152]{2,1,0:T(4,128)} %copy.56.mod, bf16[4,128,1152]{2,1,0:T(8,128)(2,1)} %bitcast.82, bf16[4,128,576]{2,1,0:T(8,128)(2,1)} %shard_map.145.out_s, bf16[4,128,576]{2,1,0:T(8,128)(2,1)} %bitcast.88, bf16[1152,576]{1,0:T(8,128)(2,1)} %get-tuple-element.47.w_spatial, ...), custom_call_target="tpu_custom_call" | custom-call | flops 1358954496 | bytes 6206992 | tf_op jit(solution)/shard_map/pallas_call | solution.py:256
  309.7 18.1 %shard_map.150 = (bf16[4,128,1152]{2,1,0:T(8,128)(2,1)}, bf16[4,128,1728]{2,1,0:T(8,128)(2,1)}) custom-call(s32[4]{0:T(128)} %pad_add_fusion.info, bf16[4,128,1152]{2,1,0:T(8,128)(2,1)} %bitcast.84, bf16[4,128,1152]{2,1,0:T(8,128)(2,1)} %bitcast.86, bf16[4,128,1728]{2,1,0:T(8,128)(2,1)} %bitcast.79, bf16[4,128,576]{2,1,0:T(8,128)(2,1)} %shard_map.145.out_s, ...), custom_call_target="tpu_custom_call" | custom-call | flops 1056964608 | bytes 8994832 | tf_op jit(solution)/shard_map/pallas_call | solution.py:256
  327.8 3.8 %copy.68 = bf16[1,4,128,1728]{2,3,1,0:T(8,128)(2,1)} copy(bf16[1,4,128,1728]{3,2,1,0:T(8,128)(2,1)} %bitcast.90) | data formatting | bytes 3538944
  (59 shorter events, 43.8 us)
Async XLA Ops:
  7.2 111.2 %all-gather.6.cloned.1.call-start = ((), (), s32[]{:S(2)}) async-start(), calls=%async_computation.10 | async-start | bytes 7299072 | tf_op jit(solution)/shard_map/all_gather | solution.py:284
  9.8 17.0 %copy-start.3 = (bf16[1,4,128,1728]{2,3,1,0:T(8,128)(2,1)S(1)}, bf16[1,4,128,1728]{2,3,1,0:T(8,128)(2,1)}, u32[]{:S(2)}) copy-start(bf16[1,4,128,1728]{2,3,1,0:T(8,128)(2,1)} %param.11) | copy-start | bytes 5308420
  39.8 5.9 %copy-start.1 = (bf16[1,4,128,1152]{3,2,1,0:T(8,128)(2,1)S(1)}, bf16[1,4,128,1152]{3,2,1,0:T(8,128)(2,1)}, u32[]{:S(2)}) copy-start(bf16[1,4,128,1152]{3,2,1,0:T(8,128)(2,1)} %param.10) | copy-start | bytes 3538948
  42.0 15.5 %all-to-all-start.1 = ((bf16[8,2,32,576]{3,2,1,0:T(8,128)(2,1)}), bf16[8,2,32,576]{3,2,1,0:T(8,128)(2,1)S(1)}, u32[]{:S(2)}, u32[]{:S(2)}) async-start(bf16[8,2,32,576]{3,2,1,0:T(8,128)(2,1)} %bitcast.77), calls=%async_computation.1 | async-start | bytes 1310720 | tf_op jit(solution)/shard_map/all_to_all | solution.py:292
  45.7 15.3 %copy-start.2 = (bf16[1,4,128,1152]{3,2,1,0:T(8,128)(2,1)S(1)}, bf16[1,4,128,1152]{3,2,1,0:T(8,128)(2,1)}, u32[]{:S(2)}) copy-start(bf16[1,4,128,1152]{3,2,1,0:T(8,128)(2,1)} %param.16) | copy-start | bytes 3538948
  57.5 4.8 %copy-start.6 = (bf16[8,2,32,576]{3,2,1,0:T(8,128)(2,1)}, bf16[8,2,32,576]{3,2,1,0:T(8,128)(2,1)S(1)}, u32[]{:S(2)}) copy-start(bf16[8,2,32,576]{3,2,1,0:T(8,128)(2,1)S(1)} %all-to-all-done.1.out_s) | copy-start | bytes 1769476
  57.5 20.9 %all-to-all-start = ((bf16[8,2,32,1152]{3,2,1,0:T(8,128)(2,1)}), bf16[8,2,32,1152]{3,2,1,0:T(8,128)(2,1)S(1)}, u32[]{:S(2)}, u32[]{:S(2)}) async-start(bf16[8,2,32,1152]{3,2,1,0:T(8,128)(2,1)} %bitcast.76), calls=%async_computation | async-start | bytes 2359296 | tf_op jit(solution)/shard_map/all_to_all | solution.py:292
  61.1 21.5 %copy-start.7 = (f32[1,3,1152]{2,0,1:T(1,128)S(1)}, f32[1,3,1152]{2,0,1:T(1,128)}, u32[]{:S(2)}) copy-start(f32[1,3,1152]{2,0,1:T(1,128)} %param.15) | copy-start | bytes 41476
  78.4 40.0 %copy-start.5 = (bf16[8,2,32,1152]{3,2,1,0:T(8,128)(2,1)}, bf16[8,2,32,1152]{3,2,1,0:T(8,128)(2,1)S(1)}, u32[]{:S(2)}) copy-start(bf16[8,2,32,1152]{3,2,1,0:T(8,128)(2,1)S(1)} %all-to-all-done.stream) | copy-start | bytes 3538948
  78.4 73.0 %all-to-all-start.3 = ((bf16[8,2,32,1152]{3,2,1,0:T(8,128)(2,1)}), bf16[8,2,32,1152]{3,2,1,0:T(8,128)(2,1)}, u32[]{:S(2)}, u32[]{:S(2)}) async-start(bf16[8,2,32,1152]{3,2,1,0:T(8,128)(2,1)} %bitcast.75), calls=%async_computation.3 | async-start | bytes 2359296 | tf_op jit(solution)/shard_map/all_to_all | solution.py:292
  170.8 10.1 %copy-start.4 = (bf16[576,1152]{1,0:T(8,128)(2,1)S(1)}, bf16[576,1152]{1,0:T(8,128)(2,1)}, u32[]{:S(2)}) copy-start(bf16[576,1152]{1,0:T(8,128)(2,1)} %get-tuple-element.26) | copy-start | bytes 3981316
  184.0 8.4 %all-to-all-start.5 = ((bf16[2,4,144,1152]{3,2,1,0:T(8,128)(2,1)}), bf16[2,4,144,1152]{3,2,1,0:T(8,128)(2,1)S(1)}, u32[]{:S(2)}, u32[]{:S(2)}) async-start(bf16[2,4,144,1152]{3,2,1,0:T(8,128)(2,1)} %copy_bitcast_fusion.1), calls=%async_computation.5 | async-start | bytes 5308416 | tf_op jit(solution)/shard_map/all_to_all | solution.py:292
  192.3 10.3 %all-to-all-start.7 = ((bf16[2,4,144,1728]{3,2,1,0:T(8,128)(2,1)}), bf16[2,4,144,1728]{3,2,1,0:T(8,128)(2,1)}, u32[]{:S(2)}, u32[]{:S(2)}) async-start(bf16[2,4,144,1728]{3,2,1,0:T(8,128)(2,1)} %bitcast.80), calls=%async_computation.7 | async-start | bytes 8257536 | tf_op jit(solution)/shard_map/all_to_all | solution.py:292
  202.6 16.1 %all-to-all-start.2 = ((bf16[8,2,32,576]{3,2,1,0:T(8,128)(2,1)}), bf16[8,2,32,576]{3,2,1,0:T(8,128)(2,1)S(1)}, u32[]{:S(2)}, u32[]{:S(2)}) async-start(bf16[8,2,32,576]{3,2,1,0:T(8,128)(2,1)} %get-tuple-element.17.out_t), calls=%async_computation.2 | async-start | bytes 1310720 | tf_op jit(solution)/shard_map/all_to_all | solution.py:292
  218.7 21.7 %all-to-all-start.6 = ((bf16[4,144,1152]{2,1,0:T(8,128)(2,1)}), bf16[4,144,1152]{2,1,0:T(8,128)(2,1)S(1)}, u32[]{:S(2)}, u32[]{:S(2)}) async-start(bf16[4,144,1152]{2,1,0:T(8,128)(2,1)} %fusion.3), calls=%async_computation.6 | async-start | bytes 2654208 | tf_op jit(solution)/shard_map/all_to_all | solution.py:292
  240.4 1.1 copy-start
  241.5 29.7 %all-to-all-start.8 = ((bf16[4,144,1728]{2,1,0:T(8,128)(2,1)}), bf16[4,144,1728]{2,1,0:T(8,128)(2,1)}, u32[]{:S(2)}, u32[]{:S(2)}) async-start(bf16[4,144,1728]{2,1,0:T(8,128)(2,1)} %fusion.2), calls=%async_computation.8 | async-start | bytes 4128768 | tf_op jit(solution)/shard_map/all_to_all | solution.py:292
  271.1 21.6 %all-to-all-start.4 = ((bf16[8,2,32,1152]{3,2,1,0:T(8,128)(2,1)}), bf16[8,2,32,1152]{3,2,1,0:T(8,128)(2,1)}, u32[]{:S(2)}, u32[]{:S(2)}) async-start(bf16[8,2,32,1152]{3,2,1,0:T(8,128)(2,1)} %get-tuple-element.22), calls=%async_computation.4 | async-start | bytes 2359296 | tf_op jit(solution)/shard_map/all_to_all | solution.py:292
  292.8 38.8 %all-to-all-start.9 = ((bf16[32,90,144]{1,2,0:T(8,128)(2,1)}), bf16[32,90,144]{1,2,0:T(8,128)(2,1)S(1)}, u32[]{:S(2)}, u32[]{:S(2)}) async-start(bf16[32,90,144]{1,2,0:T(8,128)(2,1)} %copy.66), calls=%async_computation.9 | async-start | bytes 2359296 | tf_op jit(solution)/shard_map/all_to_all | solution.py:292
Sparse Core Ops, SparseCore 0:
  25.0 93.3 all-gather.5

commit v3 on v2

--- a/solution.py
+++ b/solution.py
@@ -126,7 +126,7 @@
 
 def temporal_backward(
     info, mod, grad, qkv_ref, out_t, modulated, w_temporal, dqkv_ref, g_temporal, g_qkv,
-    q_acc, k_acc, v_acc, sum_t, sum_q, slots
+    q_acc, k_acc, v_acc, sum_t, sum_q, slots, y_count
 ):
     rows, inner = q_acc.shape
     width = w_temporal.shape[0]
@@ -142,22 +142,40 @@
     dqkv = jnp.concatenate([q_acc[...], k_acc[...], v_acc[...]], axis=1).astype(BF16)
     dqkv_ref[...] = dqkv.reshape(dqkv_ref.shape)
     part_t = dot_tn(out, branch_grad)
-    part_q = dot_tn(modulated[...].reshape(rows, width), dqkv)
+    left = modulated[...].reshape(rows, width)
+    step = width // (2 * y_count)
+    cores = [
+        jnp.concatenate(
+            [left[:, (2 * y + c) * step : (2 * y + c + 1) * step] for y in range(y_count)], axis=1
+        )
+        for c in range(2)
+    ]
+    parts_q = [dot_tn(dqkv, core) for core in cores]
 
     @pl.when(pl.program_id(0) == 0)
     def _():
         sum_t[...] = part_t
-        sum_q[...] = part_q
+        for c in range(2):
+            sum_q[c] = parts_q[c]
 
     @pl.when(pl.program_id(0) > 0)
     def _():
         sum_t[...] += part_t
-        sum_q[...] += part_q
+        for c in range(2):
+            sum_q[c] += parts_q[c]
 
     @pl.when(pl.program_id(0) == pl.num_programs(0) - 1)
     def _():
-        g_temporal[...] = sum_t[...].astype(BF16)
+        store_by_core(sum_t, g_temporal)
         g_qkv[...] = sum_q[...].astype(BF16)
+
+
+def store_by_core(total, out):
+    _, y_count, step, _ = out.shape
+    for y in range(y_count):
+        for c in range(2):
+            start = (2 * y + c) * step
+            out[c, y] = total[start : start + step].astype(BF16)
 
 
 def norm_backward(
@@ -187,7 +205,7 @@
 
     @pl.when(pl.program_id(0) == pl.num_programs(0) - 1)
     def _():
-        g_spatial[...] = sum_s[...].astype(BF16)
+        store_by_core(sum_s, g_spatial)
 
 
 def frame_keys(info_ref, rows):
@@ -269,55 +287,174 @@
     return jax.ShapeDtypeStruct(dims, dtype)
 
 
+def exchange(rows, axes):
+    return lax.all_to_all(rows, axes, 0, 0, tiled=True)
+
+
+def shift(rows, axis, hops):
+    count = lax.axis_size(axis)
+    return lax.ppermute(rows, axis, [(at, (at + hops) % count) for at in range(count)])
+
+
+def shift_both(rows, axis, hops):
+    count = lax.axis_size(axis)
+    pairs = []
+    for at in range(count):
+        pairs.append((2 * at, 2 * ((at - hops) % count)))
+        pairs.append((2 * at + 1, 2 * ((at + hops) % count) + 1))
+    return lax.ppermute(rows, (axis, "c"), pairs)
+
+
+def swap(rows):
+    return shift(rows, "c", 1)
+
+
+def copy_all(copies):
+    for copy in copies:
+        copy.start()
+    for copy in copies:
+        copy.wait()
+
+
+def place_along_z(info, own, near, mid, far, last, near_p, mid_p, far_p, out, sems):
+    place, count = info[1], out.shape[0]
+    sign = 1 - 2 * info[3]
+    moves = [(own, place), (last, lax.rem(place + count // 2, count))]
+    for hops, mine, other in ((1, near, near_p), (2, mid, mid_p), (3, far, far_p)):
+        moves.append((mine, lax.rem(place + sign * hops + count, count)))
+        moves.append((other, lax.rem(place - sign * hops + count, count)))
+    copy_all(
+        [
+            pltpu.make_async_copy(source, out.at[index], sems.at[number])
+            for number, (source, index) in enumerate(moves)
+        ]
+    )
+
+
+def place_along_x(info, own, near, near_p, part, part_p, out_s, out_q, sems):
+    place, count = info[0], out_s.shape[0]
+    sign = 1 - 2 * info[3]
+    thin = out_s.shape[1]
+    half = part.shape[0]
+    opposite = lax.rem(place + count // 2, count)
+    copies = []
+
+    def move(source, target):
+        copies.append(pltpu.make_async_copy(source, target, sems.at[len(copies)]))
+
+    for block, index in (
+        (own, place),
+        (near, lax.rem(place + sign + count, count)),
+        (near_p, lax.rem(place - sign + count, count)),
+    ):
+        move(block.at[pl.ds(0, thin)], out_s.at[index])
+        move(block.at[pl.ds(thin, 2 * half - thin)], out_q.at[index])
+    copy_all(copies)
+
+    def halves(first, second):
+        copies.clear()
+        move(first.at[pl.ds(0, thin)], out_s.at[opposite])
+        move(first.at[pl.ds(thin, half - thin)], out_q.at[opposite, pl.ds(0, half - thin)])
+        move(second, out_q.at[opposite, pl.ds(half - thin, half)])
+        copy_all(copies)
+
+    @pl.when(info[3] == 0)
+    def _():
+        halves(part, part_p)
+
+    @pl.when(info[3] != 0)
+    def _():
+        halves(part_p, part)
+
+
+def place_blocks(body, info, blocks, results, copies):
+    anywhere = pl.BlockSpec(memory_space=pl.ANY)
+    return pl.pallas_call(
+        body,
+        in_specs=[SCALARS] + [anywhere] * len(blocks),
+        out_specs=jax.tree.map(lambda _: anywhere, results),
+        out_shape=results,
+        scratch_shapes=[pltpu.SemaphoreType.DMA((copies,))],
+    )(info, *blocks)
+
+
 def weight_rows(out_spatial, qkv_temporal, out_temporal):
+    half, narrow = out_spatial.shape
     packed = jnp.concatenate(
         [jnp.concatenate([out_spatial.T, out_temporal.T], axis=1), qkv_temporal.T], axis=0
     )
-    near = lax.all_gather(packed, ("y", "c"), axis=0, tiled=False)
-    narrow = out_spatial.shape[1]
-    half = out_spatial.shape[0]
-    pair = jnp.transpose(near[:, :narrow], (1, 0, 2))
-    first = pair[:, :, :half].reshape(narrow, -1)
-    second = pair[:, :, half:].reshape(narrow, -1)
-    wide = jnp.transpose(near[:, narrow:], (1, 0, 2)).reshape(near.shape[1] - narrow, -1)
-    rows = jnp.concatenate([jnp.concatenate([first, second], axis=1), wide], axis=0)
-    far = lax.all_gather(rows, ("x", "z"), axis=0, tiled=False)
-    inner = first.shape[1]
-    w_pair = far[:, :narrow].reshape(-1, 2 * inner)
-    w_wide = far[:, narrow:].reshape(-1, far.shape[2])
-    return (w_pair[:, :inner], w_wide, w_pair[:, inner:])
-
-
-def exchange(rows, axes):
-    return lax.all_to_all(rows, axes, 0, 0, tiled=True)
-
-
-def halve_and_quarter(terms):
-    split = terms.reshape((4, 2) + terms.shape[1:])
-    split = jnp.transpose(split, (1, 0, 2, 3))
-    pairs = exchange(split, "c").astype(F32)
-    pairs = (pairs[0] + pairs[1]).astype(BF16)
-    quads = exchange(pairs, "y").astype(F32)
-    return ((quads[0] + quads[1]) + (quads[2] + quads[3])).astype(BF16)
+    near = jnp.transpose(lax.all_gather(packed, ("y", "c"), axis=0, tiled=False), (1, 0, 2))
+    thin = near[:narrow, :, :half].reshape(narrow, -1)
+    inner = thin.shape[1]
+    wide = near[narrow:].reshape(near.shape[0] - narrow, -1)
+    w_temporal = lax.all_gather(near[:narrow, :, half:].reshape(narrow, -1), ("x", "z"), axis=0)
+    w_temporal = w_temporal.reshape(-1, inner)
+
+    coords = jnp.stack([lax.axis_index(name) for name in ("x", "z", "y", "c")]).astype(jnp.int32)
+    cut = narrow // 2
+    rows = jnp.concatenate([jnp.concatenate([thin[:cut], thin[cut:]], axis=1), wide], axis=0)
+    arrived = [shift_both(rows, "z", hops) for hops in (1, 2, 3)] + [shift(rows, "z", 4)]
+    swapped = [swap(block) for block in arrived[:3]]
+    z_count, x_count = lax.axis_size("z"), lax.axis_size("x")
+    stack = place_blocks(
+        place_along_z, coords, [rows] + arrived + swapped, shape_of(z_count, *rows.shape), z_count
+    )
+    thin = jnp.concatenate([stack[:, :cut, :inner], stack[:, :cut, inner:]], axis=1)
+    thin = thin.reshape(-1, inner)
+    cut = thin.shape[0] // 2
+    wide = stack[:, narrow // 2 :].reshape(-1, stack.shape[2])
+    rows = jnp.concatenate([jnp.concatenate([thin[:cut], thin[cut:]], axis=1), wide], axis=0)
+    first = shift_both(rows, "x", 1)
+    size = rows.shape[0] // 2
+    onward = lax.dynamic_slice_in_dim(first, lax.axis_index("c") * size, size, 0)
+    second = shift_both(onward, "x", 1)
+    w_thin, w_wide = place_blocks(
+        place_along_x,
+        coords,
+        [rows, first, swap(first), second, swap(second)],
+        (
+            shape_of(x_count, cut, rows.shape[1]),
+            shape_of(x_count, wide.shape[0], rows.shape[1]),
+        ),
+        6,
+    )
+    w_thin = jnp.concatenate([w_thin[:, :, :inner], w_thin[:, :, inner:]], axis=1)
+    return (w_thin.reshape(-1, inner), w_wide.reshape(-1, rows.shape[1]), w_temporal)
+
+
+def summed_halves(terms):
+    pair = exchange(terms, "c").astype(F32)
+    return pair[0] + pair[1]
+
+
+def scatter_sum(blocks, axis):
+    count, place = lax.axis_size(axis), lax.axis_index(axis)
+    total = lax.dynamic_index_in_dim(blocks, place, 0, keepdims=False).astype(F32)
+    for hops in range(1, count):
+        block = lax.dynamic_index_in_dim(blocks, (place + hops) % count, 0, keepdims=False)
+        total = total + shift(block, axis, hops).astype(F32)
+    return total
 
 
 def reduce_grads(g_spatial, g_qkv, g_temporal):
-    seq_count = lax.axis_size(("y", "c"))
-    dp_count = lax.axis_size(("x", "z"))
-    width = g_spatial.shape[1]
-    sum_qkv = halve_and_quarter(g_qkv.reshape(seq_count, -1, g_qkv.shape[1]))
-    pair = [g.reshape(seq_count, -1, width) for g in (g_spatial, g_temporal)]
-    sum_pair = halve_and_quarter(jnp.concatenate(pair, axis=1))
+    x_count, z_count = lax.axis_size("x"), lax.axis_size("z")
+    y_count = lax.axis_size("y")
+    wide = summed_halves(g_qkv).astype(BF16)
+    wide = scatter_sum(wide.reshape(x_count, -1, wide.shape[1]), "x").astype(BF16)
+    wide = jnp.transpose(wide.reshape(wide.shape[0], y_count, -1), (1, 0, 2))
+    wide = scatter_sum(wide, "y").astype(BF16)
+
+    pair = jnp.concatenate([summed_halves(g_spatial), summed_halves(g_temporal)], axis=1)
+    pair = jnp.sum(exchange(pair.astype(BF16), "y").astype(F32), axis=0).astype(BF16)
+    pair = scatter_sum(pair.T.reshape(x_count, -1, pair.shape[0]), "x").astype(BF16)
+
     chunks = jnp.concatenate(
-        [
-            sum_pair.T.reshape(dp_count, -1, sum_pair.shape[0]),
-            sum_qkv.T.reshape(dp_count, -1, sum_qkv.shape[0]),
-        ],
+        [pair.reshape(z_count, -1, pair.shape[1]), wide.reshape(z_count, -1, wide.shape[1])],
         axis=1,
     )
-    total = jnp.sum(exchange(chunks, ("x", "z")).astype(F32), axis=0)
-    narrow = width // dp_count
-    half = sum_pair.shape[0] // 2
+    total = jnp.sum(exchange(chunks, "z").astype(F32), axis=0)
+    narrow = pair.shape[0] // z_count
+    half = pair.shape[1] // 2
     return (total[:narrow, :half].T, total[narrow:].T, total[:narrow, half:].T)
 
 
@@ -335,6 +472,7 @@
 ):
     seq_count = lax.axis_size(("y", "c"))
     seq_place = lax.axis_index(("y", "c"))
+    y_count = lax.axis_size("y")
     stream = hidden[0]
     grad_out = cotangent[0]
     packed_qkv = spatial_qkv[0]
@@ -401,22 +539,22 @@
 
     result = (
         shape_of(groups, rows, 3 * inner),
-        shape_of(inner, width),
-        shape_of(width, 3 * inner),
+        shape_of(2, y_count, inner // seq_count, width),
+        shape_of(2, 3 * inner, width // 2),
     )
     dqkv_t, g_temporal, g_qkv = run(
-        functools.partial(temporal_backward, slots=slots),
+        functools.partial(temporal_backward, slots=slots, y_count=y_count),
         groups,
         [info, modulation, grad_s, qkv_t, out_t, modulated, w_temporal],
         [SCALARS, whole(modulation), per_group(grad_s), per_frame(qkv_t), per_group(out_t), per_frame(modulated), whole(w_temporal)],
         result,
         [per_frame(result[0]), whole(result[1]), whole(result[2])],
-        [group_acc, group_acc, group_acc, pltpu.VMEM((inner, width), F32), pltpu.VMEM((width, 3 * inner), F32)],
+        [group_acc, group_acc, group_acc, pltpu.VMEM((inner, width), F32), pltpu.VMEM((2, 3 * inner, width // 2), F32)],
         10 * tokens * width * inner + 10 * tokens * rows * inner,
     )
     result = (
         shape_of(seq_count, groups, rows // seq_count, width),
-        shape_of(inner, width),
+        shape_of(2, y_count, inner // seq_count, width),
     )
     ln_grad, g_spatial = run(
         functools.partial(norm_backward, slots=slots),

time: 343 us -> 561 us (1.64)
  Pallas kernels: 76.2 us -> 283 us
  waiting for transfers between devices: 112 us -> 76.6 us
  starting transfers between devices: 44.3 us -> 72.7 us
  blocking collectives: 13.5 us -> 27.9 us
    pallas_call x0 -> x2, Pallas kernels: none -> 206 us  [place_blocks(): pl.pallas_call(body, in_specs=[SCALARS] + [anywhere] * len(blocks), out_s...]
    all_to_all x10 -> x9, waiting for transfers between devices: 76.3 us -> 22.2 us  [exchange(): return lax.all_to_all(rows, axes, 0, 0, tiled=True)]
    ppermute x0 -> x20, waiting for transfers between devices: none -> 43.5 us  [the longest x5 24 us: shift_both(): return lax.ppermute(rows, (axis, 'c'), pairs)]
    ppermute x0 -> x20, starting transfers between devices: none -> 31.9 us  [the longest x15 20.7 us: shift(): lax.ppermute(rows, axis, [(at, (at + hops) % count) for at in range(count)])]
    all_gather x1, waiting for transfers between devices: 35.2 us -> 10.9 us  [weight_rows(): lax.all_gather(near[:narrow, :, half:].reshape(narrow, -1), ('x', 'z'), a...]
    all_to_all x0 -> x1, blocking collectives: none -> 14.5 us  [exchange(): return lax.all_to_all(rows, axes, 0, 0, tiled=True)]
    reshape x7, local copies, waits for them, and re-layouts: 17.9 us -> 5.01 us  [the longest x1 3.57 us: weight_rows(): w_temporal = w_temporal.reshape(-1, inner)]
    slice x5 -> x10, local copies, waits for them, and re-layouts: 12.9 us -> 5.04 us  [the longest x1 1.74 us: weight_rows(): w_thin[:, :, :inner]]
  transfers between devices with their start and end apart: 11 -> 30, of which waited for: 8 -> 13; matrix products, arithmetic and copies ran while one was open for 20% -> 12% of each run, Pallas kernels for 14% -> 38%
where the time goes in v3:
time: 561 us; the launch traced here: 554 us
  Pallas kernels  283 us (50%)
  waiting for transfers between devices  76.6 us (14%)
  starting transfers between devices  72.7 us (13%)
  local copies, waits for them, and re-layouts  56.6 us (10%)
  blocking collectives  27.9 us (5%)
  other arithmetic  21.3 us (4%)
  between operations  16.7 us (3%)
    pallas_call x2, Pallas kernels, place_blocks(): pl.pallas_call(body, in_specs=[SCALARS] + [anywhere] * len(blocks), out_s...  206 us
    pallas_call x6, Pallas kernels, run(): pl.pallas_call(body, grid=(steps,), in_specs=specs, out_specs=result_spec...  76.8 us
    all_to_all x9, starting transfers between devices, exchange(): return lax.all_to_all(rows, axes, 0, 0, tiled=True)  40.8 us
    ppermute x5, waiting for transfers between devices, shift_both(): return lax.ppermute(rows, (axis, 'c'), pairs)  24 us
    all_to_all x9, waiting for transfers between devices, exchange(): return lax.all_to_all(rows, axes, 0, 0, tiled=True)  22.2 us
    ppermute x15, starting transfers between devices, shift(): lax.ppermute(rows, axis, [(at, (at + hops) % count) for at in range(count)])  20.7 us
    ppermute x15, waiting for transfers between devices, shift(): lax.ppermute(rows, axis, [(at, (at + hops) % count) for at in range(count)])  19.4 us
    unnamed x46, local copies, waits for them, and re-layouts  17.5 us
  transfers between devices with their start and end apart: 30, of which 13 were waited for; matrix products, arithmetic and copies ran while one was open for 12% of the time, Pallas kernels for 38%

profile of v3, /device:TPU:32, one launch (start us, length us, event | category | flops | bytes accessed | tf_op | source)
XLA Modules:
  0.0 554.4 jit_solution(8194050667737653673)
XLA Ops:
  9.8 13.4 %all-gather.1 = bf16[8,90,144]{1,2,0:T(8,128)(2,1)S(1)} all-gather(bf16[1,90,144]{1,2,0:T(8,128)(2,1)S(1)} %maximum_bitcast_fusion), channel_id=2, replica_groups=mesh['x'=4,'z'=8,'y'=4,'c'=2] {'y','c'}, dimensions={0}, use_global_device_ids=true | all-gather | bytes 233280 | tf_op jit(solution)/shard_map/all_gather | solution.py:386
  25.4 5.1 collective-permute-start.1
  31.5 4.5 collective-permute-start.3
  36.0 4.4 collective-permute-done.1.mid
  40.5 5.4 collective-permute-done.2.far
  46.5 4.6 collective-permute-done.3.last
  52.6 42.0 %shard_map.146 = bf16[8,72,1152]{2,1,0:T(8,128)(2,1)} custom-call(s32[4]{0:T(128)} %pad_add_fusion.1.info, bf16[72,1152]{1,0:T(8,128)(2,1)} %copy-done.7, bf16[72,1152]{1,0:T(8,128)(2,1)} %copy-done.10, bf16[72,1152]{1,0:T(8,128)(2,1)} %copy-done.11, bf16[72,1152]{1,0:T(8,128)(2,1)} %copy-done.12, bf16[72,1152]{1,0:T(8,128)(2,1)} %copy-done.13, ...), custom_call_target="tpu_custom_call" | custom-call | tf_op jit(solution)/shard_map/pallas_call | solution.py:372
  103.5 3.8 copy.82
  108.0 9.8 %shard_map.145.out_s = bf16[4,128,576]{2,1,0:T(8,128)(2,1)} custom-call(s32[4]{0:T(128)} %pad_add_fusion.info, bf16[4,128,1728]{2,1,0:T(8,128)(2,1)} %bitcast.91), custom_call_target="tpu_custom_call" | custom-call | flops 150994944 | bytes 2359312 | tf_op jit(solution)/shard_map/pallas_call | solution.py:274
  124.8 10.6 %all-to-all-done.1.out_s = bf16[8,2,32,576]{3,2,1,0:T(8,128)(2,1)S(1)} async-done(((bf16[8,2,32,576]{3,2,1,0:T(8,128)(2,1)}), bf16[8,2,32,576]{3,2,1,0:T(8,128)(2,1)S(1)}, u32[]{:S(2)}, u32[]{:S(2)}) %all-to-all-start.1) | async-done | bytes 589856 | tf_op jit(solution)/shard_map/all_to_all | solution.py:291
  135.4 4.4 all-to-all-start
  141.9 14.2 %collective-permute-done.9.part = bf16[288,1152]{1,0:T(8,128)(2,1)S(1)} collective-permute-done((bf16[288,1152]{1,0:T(8,128)(2,1)S(1)}, bf16[288,1152]{1,0:T(8,128)(2,1)S(1)}, u32[]{:S(2)}, u32[]{:S(2)}) %collective-permute-start.9) | collective-permute-done | bytes 663584 | tf_op jit(solution)/shard_map/ppermute | solution.py:305
  158.2 4.7 all-to-all-start.3
  163.5 10.9 %all-gather.4.cloned.1.call-done = bf16[32,36,576]{2,1,0:T(8,128)(2,1)} async-done(((bf16[1,36,576]{2,1,0:T(8,128)(2,1)}), bf16[32,36,576]{2,1,0:T(8,128)(2,1)}) %all-gather.4.cloned.1.call-update) | async-done | bytes 1327120 | tf_op jit(solution)/shard_map/all_gather | solution.py:390
  179.1 163.7 %shard_map.147 = (bf16[4,144,1152]{2,1,0:T(8,128)(2,1)}, bf16[4,432,1152]{2,1,0:T(8,128)(2,1)}) custom-call(s32[4]{0:T(128)} %pad_add_fusion.1.info, bf16[576,1152]{1,0:T(8,128)(2,1)} %copy-done, bf16[576,1152]{1,0:T(8,128)(2,1)} %collective-permute-done.7.near, bf16[576,1152]{1,0:T(8,128)(2,1)} %copy-done.5, bf16[288,1152]{1,0:T(8,128)(2,1)} %copy-done.8, ...), custom_call_target="tpu_custom_call" | custom-call | tf_op jit(solution)/shard_map/pallas_call | solution.py:372
  345.8 11.6 %shard_map.148 = (bf16[2,256,1152]{2,1,0:T(8,128)(2,1)}, bf16[2,256,1152]{2,1,0:T(8,128)(2,1)}, bf16[2,256,1728]{2,1,0:T(8,128)(2,1)}, bf16[8,2,32,576]{3,2,1,0:T(8,128)(2,1)}) custom-call(s32[4]{0:T(128)} %pad_add_fusion.info, f32[1,3,1152]{2,1,0:T(4,128)} %copy.94.mod, bf16[8,2,32,1152]{3,2,1,0:T(8,128)(2,1)} %all-to-all-done.stream, ...), custom_call_target="tpu_custom_call" | custom-call | flops 3019898880 | bytes 11810320 | tf_op jit(solution)/shard_map/pallas_call | solution.py:274
  358.5 20.2 %shard_map.150 = (bf16[2,256,1728]{2,1,0:T(8,128)(2,1)}, bf16[2,4,72,1152]{3,2,1,0:T(8,128)(2,1)}, bf16[2,1728,576]{2,1,0:T(8,128)(2,1)}) custom-call(s32[4]{0:T(128)} %pad_add_fusion.info, f32[1,3,1152]{2,1,0:T(4,128)} %copy.94.mod, bf16[8,2,32,1152]{3,2,1,0:T(8,128)(2,1)} %copy-done.6, bf16[2,256,1728]{2,1,0:T(8,128)(2,1)} %get-tuple-element.23.qkv_ref, ...), custom_call_target="tpu_custom_call" | custom-call | flops 4152360960 | bytes 13137424 | tf_op jit(solution)/shard_map/pallas_call | solution.py:274
  378.7 9.9 %shard_map.151 = (bf16[8,2,32,1152]{3,2,1,0:T(8,128)(2,1)}, bf16[2,4,72,1152]{3,2,1,0:T(8,128)(2,1)}) custom-call(s32[4]{0:T(128)} %pad_add_fusion.info, f32[1,3,1152]{2,1,0:T(4,128)} %copy.94.mod, bf16[8,2,32,1152]{3,2,1,0:T(8,128)(2,1)} %copy-done.6, bf16[2,256,1152]{2,1,0:T(8,128)(2,1)} %get-tuple-element.22.mixed, bf16[8,2,32,576]{3,2,1,0:T(8,128)(2,1)} %copy-done.9, ...), custom_call_target="tpu_custom_call" | custom-call | flops 2717908992 | bytes 11220496 | tf_op jit(solution)/shard_map/pallas_call | solution.py:274
  388.6 14.5 %all_to_all.50 = bf16[2,4,72,1152]{3,2,1,0:T(8,128)(2,1)S(1)} all-to-all(bf16[2,4,72,1152]{3,2,1,0:T(8,128)(2,1)} %get-tuple-element.29), channel_id=1, replica_groups=mesh['x'=4,'z'=8,'y'=4,'c'=2] {'c'}, dimensions={0} | all-to-all | bytes 2654208 | tf_op jit(solution)/shard_map/all_to_all | solution.py:291
  407.2 6.4 %copy.103 = bf16[2,1728,576]{1,2,0:T(8,128)(2,1)} copy(bf16[2,1728,576]{2,1,0:T(8,128)(2,1)} %get-tuple-element.31) | data formatting | bytes 7962624 | tf_op jit(solution)/shard_map/pallas_call | solution.py:274
  414.7 5.6 %all-to-all-start.8 = ((bf16[2,1728,576]{1,2,0:T(8,128)(2,1)}), bf16[2,1728,576]{1,2,0:T(8,128)(2,1)}, u32[]{:S(2)}, u32[]{:S(2)}) async-start(bf16[2,1728,576]{1,2,0:T(8,128)(2,1)} %copy.103), calls=%async_computation.8 | async-start | bytes 8257536 | tf_op jit(solution)/shard_map/all_to_all | solution.py:291
  424.7 4.2 all-to-all-start.2
  429.8 6.3 %copy.104 = bf16[2,1728,576]{2,1,0:T(8,128)(2,1)} copy(bf16[2,1728,576]{1,2,0:T(8,128)(2,1)} %all-to-all-done.8) | data formatting | bytes 7962624 | tf_op jit(solution)/shard_map/all_to_all | solution.py:291
  436.2 6.4 %convert_element_type.84 = f32[2,1728,576]{2,1,0:T(8,128)} convert(bf16[2,1728,576]{2,1,0:T(8,128)(2,1)} %copy.104) | non-fusion elementwise | flops 1990656 | bytes 11943936 | tf_op jit(solution)/shard_map/convert_element_type | solution.py:426
  443.7 4.7 all-to-all-start.7
  448.4 4.0 fusion
  458.1 8.7 %all-to-all-done.7 = bf16[4,144,1152]{2,1,0:T(8,128)(2,1)S(1)} async-done(((bf16[4,144,1152]{2,1,0:T(8,128)(2,1)}), bf16[4,144,1152]{2,1,0:T(8,128)(2,1)S(1)}, u32[]{:S(2)}, u32[]{:S(2)}) %all-to-all-start.7) | async-done | bytes 1327136 | tf_op jit(solution)/shard_map/all_to_all | solution.py:291
  466.8 4.3 all-to-all-start.4
  471.1 10.3 %collective-permute-done.14 = bf16[432,576]{1,0:T(8,128)(2,1)} collective-permute-done((bf16[432,576]{1,0:T(8,128)(2,1)}, bf16[432,576]{1,0:T(8,128)(2,1)}, u32[]{:S(2)}, u32[]{:S(2)}) %collective-permute-start.14) | collective-permute-done | bytes 497696 | tf_op jit(solution)/shard_map/ppermute | solution.py:296
  506.1 5.6 %all-to-all-start.9 = ((bf16[8,90,144]{1,2,0:T(8,128)(2,1)}), bf16[8,90,144]{1,2,0:T(8,128)(2,1)S(1)}, u32[]{:S(2)}, u32[]{:S(2)}) async-start(bf16[8,90,144]{1,2,0:T(8,128)(2,1)} %copy.107), calls=%async_computation.9 | async-start | bytes 589824 | tf_op jit(solution)/shard_map/all_to_all | solution.py:291
  513.7 7.2 %shard_map.149 = bf16[4,128,1152]{2,1,0:T(8,128)(2,1)} custom-call(s32[4]{0:T(128)} %pad_add_fusion.info, f32[1,3,1152]{2,1,0:T(4,128)} %copy.94.mod, bf16[4,128,1152]{2,1,0:T(8,128)(2,1)} %bitcast.99, bf16[4,128,576]{2,1,0:T(8,128)(2,1)} %shard_map.145.out_s, bf16[4,128,576]{2,1,0:T(8,128)(2,1)} %bitcast.108, bf16[1152,576]{1,0:T(8,128)(2,1)} %bitcast.94, ...), custom_call_target="tpu_custom_call" | custom-call | flops 1358954496 | bytes 6206992 | tf_op jit(solution)/shard_map/pallas_call | solution.py:274
  523.2 18.1 %shard_map.152 = (bf16[4,128,1152]{2,1,0:T(8,128)(2,1)}, bf16[4,128,1728]{2,1,0:T(8,128)(2,1)}) custom-call(s32[4]{0:T(128)} %pad_add_fusion.info, bf16[4,128,1152]{2,1,0:T(8,128)(2,1)} %bitcast.101, bf16[4,128,1152]{2,1,0:T(8,128)(2,1)} %bitcast.103, bf16[4,128,1728]{2,1,0:T(8,128)(2,1)} %bitcast.92, bf16[4,128,576]{2,1,0:T(8,128)(2,1)} %shard_map.145.out_s, ...), custom_call_target="tpu_custom_call" | custom-call | flops 1056964608 | bytes 8994832 | tf_op jit(solution)/shard_map/pallas_call | solution.py:274
  (141 shorter events, 88.2 us)
Async XLA Ops:
  7.2 167.3 %all-gather.4.cloned.1.call-start = ((), (), s32[]{:S(2)}) async-start(), calls=%async_computation.10 | async-start | bytes 1689600 | tf_op jit(solution)/shard_map/all_gather | solution.py:390
  24.0 27.1 %copy-start.7 = (bf16[72,1152]{1,0:T(8,128)(2,1)}, bf16[72,1152]{1,0:T(8,128)(2,1)S(1)}, u32[]{:S(2)}) copy-start(bf16[72,1152]{1,0:T(8,128)(2,1)S(1)} %fusion.16.own) | copy-start | bytes 497668
  24.0 12.0 %collective-permute-start = (bf16[72,1152]{1,0:T(8,128)(2,1)S(1)}, bf16[72,1152]{1,0:T(8,128)(2,1)S(1)}, u32[]{:S(2)}, u32[]{:S(2)}) collective-permute-start(bf16[72,1152]{1,0:T(8,128)(2,1)S(1)} %fusion.16.own), channel_id=1, source_target_pairs={{0,56},{1,9},{8,0},{9,17},{16,8},{17,25},{24,16},{25,33},{32,24},{... | collective-permute-start | bytes 497672 | tf_op jit(solution)/shard_map/ppermute | solution.py:305
  25.4 15.0 %collective-permute-start.1 = (bf16[72,1152]{1,0:T(8,128)(2,1)S(1)}, bf16[72,1152]{1,0:T(8,128)(2,1)S(1)}, u32[]{:S(2)}, u32[]{:S(2)}) collective-permute-start(bf16[72,1152]{1,0:T(8,128)(2,1)S(1)} %fusion.16.own), channel_id=1, source_target_pairs={{0,48},{1,17},{8,56},{9,25},{16,0},{17,33},{24,8},{25,41},{32,16},... | collective-permute-start | bytes 497672 | tf_op jit(solution)/shard_map/ppermute | solution.py:305
  30.5 15.3 %collective-permute-start.2 = (bf16[72,1152]{1,0:T(8,128)(2,1)S(1)}, bf16[72,1152]{1,0:T(8,128)(2,1)S(1)}, u32[]{:S(2)}, u32[]{:S(2)}) collective-permute-start(bf16[72,1152]{1,0:T(8,128)(2,1)S(1)} %fusion.16.own), channel_id=1, source_target_pairs={{0,40},{1,25},{8,48},{9,33},{16,56},{17,41},{24,0},{25,49},{32,8},... | collective-permute-start | bytes 497672 | tf_op jit(solution)/shard_map/ppermute | solution.py:305
  31.5 19.6 %collective-permute-start.3 = (bf16[72,1152]{1,0:T(8,128)(2,1)S(1)}, bf16[72,1152]{1,0:T(8,128)(2,1)S(1)}, u32[]{:S(2)}, u32[]{:S(2)}) collective-permute-start(bf16[72,1152]{1,0:T(8,128)(2,1)S(1)} %fusion.16.own), channel_id=1, source_target_pairs={{0,32},{8,40},{16,48},{24,56},{32,0},{40,8},{48,16},{56,24},{1,33}... | collective-permute-start | bytes 497672 | tf_op jit(solution)/shard_map/ppermute | solution.py:296
  36.0 15.1 %collective-permute-start.4 = (bf16[72,1152]{1,0:T(8,128)(2,1)S(1)}, bf16[72,1152]{1,0:T(8,128)(2,1)S(1)}, u32[]{:S(2)}, u32[]{:S(2)}) collective-permute-start(bf16[72,1152]{1,0:T(8,128)(2,1)S(1)} %collective-permute-done.near), channel_id=1, source_target_pairs={{0,1},{1,0},{2,3},{3,2},{4,5},{5,4},{6,7},{7,6},{8,9},{9,8},{10,11... | collective-permute-start | bytes 497672 | tf_op jit(solution)/shard_map/ppermute | solution.py:296
  40.4 10.7 %collective-permute-start.5 = (bf16[72,1152]{1,0:T(8,128)(2,1)S(1)}, bf16[72,1152]{1,0:T(8,128)(2,1)S(1)}, u32[]{:S(2)}, u32[]{:S(2)}) collective-permute-start(bf16[72,1152]{1,0:T(8,128)(2,1)S(1)} %collective-permute-done.1.mid), channel_id=1, source_target_pairs={{0,1},{1,0},{2,3},{3,2},{4,5},{5,4},{6,7},{7,6},{8,9},{9,8},{10,11... | collective-permute-start | bytes 497672 | tf_op jit(solution)/shard_map/ppermute | solution.py:296
  45.8 5.3 collective-permute-start.6
  97.9 41.9 %collective-permute-start.7 = (bf16[576,1152]{1,0:T(8,128)(2,1)S(1)}, bf16[576,1152]{1,0:T(8,128)(2,1)}, u32[]{:S(2)}, u32[]{:S(2)}) collective-permute-start(bf16[576,1152]{1,0:T(8,128)(2,1)S(1)} %fusion.3.own), channel_id=1, source_target_pairs={{0,192},{1,65},{64,0},{65,129},{128,64},{129,193},{192,128},{193,1... | collective-permute-start | bytes 3981320 | tf_op jit(solution)/shard_map/ppermute | solution.py:305
  119.9 15.5 %all-to-all-start.1 = ((bf16[8,2,32,576]{3,2,1,0:T(8,128)(2,1)}), bf16[8,2,32,576]{3,2,1,0:T(8,128)(2,1)S(1)}, u32[]{:S(2)}, u32[]{:S(2)}) async-start(bf16[8,2,32,576]{3,2,1,0:T(8,128)(2,1)} %bitcast.90), calls=%async_computation.1 | async-start | bytes 1310720 | tf_op jit(solution)/shard_map/all_to_all | solution.py:291
  135.4 21.5 %copy-start.3 = (bf16[1,4,128,1152]{3,2,1,0:T(8,128)(2,1)S(1)}, bf16[1,4,128,1152]{3,2,1,0:T(8,128)(2,1)}, u32[]{:S(2)}) copy-start(bf16[1,4,128,1152]{3,2,1,0:T(8,128)(2,1)} %param.16) | copy-start | bytes 3538948
  135.4 22.8 %all-to-all-start = ((bf16[8,2,32,1152]{3,2,1,0:T(8,128)(2,1)}), bf16[8,2,32,1152]{3,2,1,0:T(8,128)(2,1)}, u32[]{:S(2)}, u32[]{:S(2)}) async-start(bf16[8,2,32,1152]{3,2,1,0:T(8,128)(2,1)} %bitcast.104), calls=%async_computation | async-start | bytes 2359296 | tf_op jit(solution)/shard_map/all_to_all | solution.py:291
  141.0 15.1 %collective-permute-start.9 = (bf16[288,1152]{1,0:T(8,128)(2,1)S(1)}, bf16[288,1152]{1,0:T(8,128)(2,1)S(1)}, u32[]{:S(2)}, u32[]{:S(2)}) collective-permute-start(bf16[288,1152]{1,0:T(8,128)(2,1)S(1)} %constant_dynamic-slice_fusion.4), channel_id=1, source_target_pairs={{0,192},{1,65},{64,0},{65,129},{128,64},{129,193},{192,128},{193,1... | collective-permute-start | bytes 1990664 | tf_op jit(solution)/shard_map/ppermute | solution.py:305
  141.9 36.2 %collective-permute-start.8 = (bf16[576,1152]{1,0:T(8,128)(2,1)}, bf16[576,1152]{1,0:T(8,128)(2,1)S(1)}, u32[]{:S(2)}, u32[]{:S(2)}) collective-permute-start(bf16[576,1152]{1,0:T(8,128)(2,1)} %collective-permute-done.7.near), channel_id=1, source_target_pairs={{0,1},{1,0},{2,3},{3,2},{4,5},{5,4},{6,7},{7,6},{8,9},{9,8},{10,11... | collective-permute-start | bytes 3981320 | tf_op jit(solution)/shard_map/ppermute | solution.py:296
  156.1 21.9 %collective-permute-start.10 = (bf16[288,1152]{1,0:T(8,128)(2,1)S(1)}, bf16[288,1152]{1,0:T(8,128)(2,1)}, u32[]{:S(2)}, u32[]{:S(2)}) collective-permute-start(bf16[288,1152]{1,0:T(8,128)(2,1)S(1)} %collective-permute-done.9.part), channel_id=1, source_target_pairs={{0,1},{1,0},{2,3},{3,2},{4,5},{5,4},{6,7},{7,6},{8,9},{9,8},{10,11... | collective-permute-start | bytes 1990664 | tf_op jit(solution)/shard_map/ppermute | solution.py:296
  158.2 199.3 %all-to-all-start.3 = ((bf16[8,2,32,1152]{3,2,1,0:T(8,128)(2,1)}), bf16[8,2,32,1152]{3,2,1,0:T(8,128)(2,1)S(1)}, u32[]{:S(2)}, u32[]{:S(2)}) async-start(bf16[8,2,32,1152]{3,2,1,0:T(8,128)(2,1)} %bitcast.88), calls=%async_computation.3 | async-start | bytes 2359296 | tf_op jit(solution)/shard_map/all_to_all | solution.py:291
  403.5 10.1 %all-to-all-start.6 = ((bf16[2,4,72,1152]{3,2,1,0:T(8,128)(2,1)}), bf16[2,4,72,1152]{3,2,1,0:T(8,128)(2,1)S(1)}, u32[]{:S(2)}, u32[]{:S(2)}) async-start(bf16[2,4,72,1152]{3,2,1,0:T(8,128)(2,1)} %get-tuple-element.30), calls=%async_computation.6 | async-start | bytes 2654208 | tf_op jit(solution)/shard_map/all_to_all | solution.py:291
  414.7 10.0 %all-to-all-start.8 = ((bf16[2,1728,576]{1,2,0:T(8,128)(2,1)}), bf16[2,1728,576]{1,2,0:T(8,128)(2,1)}, u32[]{:S(2)}, u32[]{:S(2)}) async-start(bf16[2,1728,576]{1,2,0:T(8,128)(2,1)} %copy.103), calls=%async_computation.8 | async-start | bytes 8257536 | tf_op jit(solution)/shard_map/all_to_all | solution.py:291
  424.7 19.0 %all-to-all-start.2 = ((bf16[8,2,32,576]{3,2,1,0:T(8,128)(2,1)}), bf16[8,2,32,576]{3,2,1,0:T(8,128)(2,1)}, u32[]{:S(2)}, u32[]{:S(2)}) async-start(bf16[8,2,32,576]{3,2,1,0:T(8,128)(2,1)} %get-tuple-element.21.out_t), calls=%async_computation.2 | async-start | bytes 1310720 | tf_op jit(solution)/shard_map/all_to_all | solution.py:291
  443.7 23.1 %all-to-all-start.7 = ((bf16[4,144,1152]{2,1,0:T(8,128)(2,1)}), bf16[4,144,1152]{2,1,0:T(8,128)(2,1)S(1)}, u32[]{:S(2)}, u32[]{:S(2)}) async-start(bf16[4,144,1152]{2,1,0:T(8,128)(2,1)} %pad_maximum_fusion.2), calls=%async_computation.7 | async-start | bytes 2654208 | tf_op jit(solution)/shard_map/all_to_all | solution.py:291
  453.6 27.7 %collective-permute-start.14 = (bf16[432,576]{1,0:T(8,128)(2,1)}, bf16[432,576]{1,0:T(8,128)(2,1)}, u32[]{:S(2)}, u32[]{:S(2)}) collective-permute-start(bf16[432,576]{1,0:T(8,128)(2,1)} %get-tuple-element.56), channel_id=1, source_target_pairs={{0,64},{64,128},{128,192},{192,0},{1,65},{65,129},{129,193},{193,1... | collective-permute-start | bytes 1493000 | tf_op jit(solution)/shard_map/ppermute | solution.py:296
  454.1 27.2 %collective-permute-start.15 = (bf16[432,576]{1,0:T(8,128)(2,1)}, bf16[432,576]{1,0:T(8,128)(2,1)}, u32[]{:S(2)}, u32[]{:S(2)}) collective-permute-start(bf16[432,576]{1,0:T(8,128)(2,1)} %get-tuple-element.58), channel_id=1, source_target_pairs={{0,128},{64,192},{128,0},{192,64},{1,129},{65,193},{129,1},{193,65... | collective-permute-start | bytes 1493000 | tf_op jit(solution)/shard_map/ppermute | solution.py:296
  456.7 25.2 %collective-permute-start.16 = (bf16[432,576]{1,0:T(8,128)(2,1)}, bf16[432,576]{1,0:T(8,128)(2,1)}, u32[]{:S(2)}, u32[]{:S(2)}) collective-permute-start(bf16[432,576]{1,0:T(8,128)(2,1)} %get-tuple-element.57), channel_id=1, source_target_pairs={{0,192},{64,0},{128,64},{192,128},{1,193},{65,1},{129,65},{193,129... | collective-permute-start | bytes 1493000 | tf_op jit(solution)/shard_map/ppermute | solution.py:296
  466.8 39.3 %all-to-all-start.4 = ((bf16[8,2,32,1152]{3,2,1,0:T(8,128)(2,1)}), bf16[8,2,32,1152]{3,2,1,0:T(8,128)(2,1)}, u32[]{:S(2)}, u32[]{:S(2)}) async-start(bf16[8,2,32,1152]{3,2,1,0:T(8,128)(2,1)} %get-tuple-element.26), calls=%async_computation.4 | async-start | bytes 2359296 | tf_op jit(solution)/shard_map/all_to_all | solution.py:291
  486.5 12.2 %collective-permute-start.17 = (bf16[432,144]{0,1:T(8,128)(2,1)}, bf16[432,144]{0,1:T(8,128)(2,1)S(1)}, u32[]{:S(2)}, u32[]{:S(2)}) collective-permute-start(bf16[432,144]{0,1:T(8,128)(2,1)} %get-tuple-element.63), channel_id=1, source_target_pairs={{0,2},{2,4},{4,6},{6,0},{1,3},{3,5},{5,7},{7,1},{8,10},{10,12},{12... | collective-permute-start | bytes 373256 | tf_op jit(solution)/shard_map/ppermute | solution.py:296
  488.2 11.2 %collective-permute-start.18 = (bf16[432,144]{0,1:T(8,128)(2,1)}, bf16[432,144]{0,1:T(8,128)(2,1)S(1)}, u32[]{:S(2)}, u32[]{:S(2)}) collective-permute-start(bf16[432,144]{0,1:T(8,128)(2,1)} %get-tuple-element.65), channel_id=1, source_target_pairs={{0,4},{2,6},{4,0},{6,2},{1,5},{3,7},{5,1},{7,3},{8,12},{10,14},{12... | collective-permute-start | bytes 373256 | tf_op jit(solution)/shard_map/ppermute | solution.py:296
  490.9 8.5 %collective-permute-start.19 = (bf16[432,144]{0,1:T(8,128)(2,1)}, bf16[432,144]{0,1:T(8,128)(2,1)}, u32[]{:S(2)}, u32[]{:S(2)}) collective-permute-start(bf16[432,144]{0,1:T(8,128)(2,1)} %get-tuple-element.64), channel_id=1, source_target_pairs={{0,6},{2,0},{4,2},{6,4},{1,7},{3,1},{5,3},{7,5},{8,14},{10,8},{12,... | collective-permute-start | bytes 373256 | tf_op jit(solution)/shard_map/ppermute | solution.py:296
  494.1 7.6 %collective-permute-start.11 = (bf16[288,144]{1,0:T(8,128)(2,1)S(1)}, bf16[288,144]{1,0:T(8,128)(2,1)S(1)}, u32[]{:S(2)}, u32[]{:S(2)}) collective-permute-start(bf16[288,144]{1,0:T(8,128)(2,1)S(1)} %bitcast.119), channel_id=1, source_target_pairs={{0,64},{64,128},{128,192},{192,0},{1,65},{65,129},{129,193},{193,1... | collective-permute-start | bytes 248840 | tf_op jit(solution)/shard_map/ppermute | solution.py:296
  495.6 8.8 %collective-permute-start.12 = (bf16[288,144]{1,0:T(8,128)(2,1)S(1)}, bf16[288,144]{1,0:T(8,128)(2,1)S(1)}, u32[]{:S(2)}, u32[]{:S(2)}) collective-permute-start(bf16[288,144]{1,0:T(8,128)(2,1)S(1)} %bitcast.120), channel_id=1, source_target_pairs={{0,128},{64,192},{128,0},{192,64},{1,129},{65,193},{129,1},{193,65... | collective-permute-start | bytes 248840 | tf_op jit(solution)/shard_map/ppermute | solution.py:296
  498.7 6.1 %collective-permute-start.13 = (bf16[288,144]{1,0:T(8,128)(2,1)S(1)}, bf16[288,144]{1,0:T(8,128)(2,1)S(1)}, u32[]{:S(2)}, u32[]{:S(2)}) collective-permute-start(bf16[288,144]{1,0:T(8,128)(2,1)S(1)} %bitcast.121), channel_id=1, source_target_pairs={{0,192},{64,0},{128,64},{192,128},{1,193},{65,1},{129,65},{193,129... | collective-permute-start | bytes 248840 | tf_op jit(solution)/shard_map/ppermute | solution.py:296
  506.1 39.0 %all-to-all-start.9 = ((bf16[8,90,144]{1,2,0:T(8,128)(2,1)}), bf16[8,90,144]{1,2,0:T(8,128)(2,1)S(1)}, u32[]{:S(2)}, u32[]{:S(2)}) async-start(bf16[8,90,144]{1,2,0:T(8,128)(2,1)} %copy.107), calls=%async_computation.9 | async-start | bytes 589824 | tf_op jit(solution)/shard_map/all_to_all | solution.py:291
  (16 other events, 70.1 us)
Sparse Core Ops, SparseCore 0:
  101.7 72.7 all-gather.3
